TPU v7x, 128 devices: a whole 4x4x4 slice. The times are simulated.
128 devices in a mesh: fsdp: 16 (over z, y), tp: 2 (over core), rep: 4 (over x).
Axes of the slice: x: 4, y: 4, z: 4, core: 2. Of those that a mesh axis runs over, the one named last changes fastest.
Arguments:
- out_momentum: float32 [5120, 5120], P(('fsdp', 'rep'), 'tp'), may hold values from -80 to 80
- out_gradient: bfloat16 [5120, 5120], P(('fsdp', 'rep'), 'tp'), may hold values from -6 to 6
- out_weight: bfloat16 [5120, 5120], P(('fsdp', 'rep'), 'tp'), may hold values from -0.078125 to 0.078125
- out_right: float32 [5120, 128], P('tp'), may hold values from -0.078125 to 0.078125
- up_momentum: float32 [5120, 13824], P(('fsdp', 'rep'), 'tp'), may hold values from -80 to 80
- up_gradient: bfloat16 [5120, 13824], P(('fsdp', 'rep'), 'tp'), may hold values from -6 to 6
- up_weight: bfloat16 [5120, 13824], P(('fsdp', 'rep'), 'tp'), may hold values from -0.078125 to 0.078125
- up_right: float32 [13824, 128], P('tp'), may hold values from -0.0546875 to 0.0546875
- down_momentum: float32 [13824, 5120], P(('fsdp', 'rep'), 'tp'), may hold values from -80 to 80
- down_gradient: bfloat16 [13824, 5120], P(('fsdp', 'rep'), 'tp'), may hold values from -6 to 6
- down_weight: bfloat16 [13824, 5120], P(('fsdp', 'rep'), 'tp'), may hold values from -0.0546875 to 0.0546875
- down_right: float32 [5120, 128], P('tp'), may hold values from -0.078125 to 0.078125
Outputs:
- out_momentum_next: float32 [5120, 5120], P(('fsdp', 'rep'), 'tp')
- up_momentum_next: float32 [5120, 13824], P(('fsdp', 'rep'), 'tp')
- down_momentum_next: float32 [13824, 5120], P(('fsdp', 'rep'), 'tp')
- out_weight_next: bfloat16 [5120, 5120], P(('fsdp', 'rep'), 'tp')
- up_weight_next: bfloat16 [5120, 13824], P(('fsdp', 'rep'), 'tp')
- down_weight_next: bfloat16 [13824, 5120], P(('fsdp', 'rep'), 'tp')
- out_right_next: float32 [5120, 128], P('tp')
- up_right_next: float32 [13824, 128], P('tp')
- down_right_next: float32 [5120, 128], P('tp')
- out_update: float32 [5120, 5120], P(('fsdp', 'rep'), 'tp')
- up_update: float32 [5120, 13824], P(('fsdp', 'rep'), 'tp')
- down_update: float32 [13824, 5120], P(('fsdp', 'rep'), 'tp')
All inputs are finite; a program needn't handle non-finite values.
Results may differ from a plain program's by a relative error of at most 0.001.
Values sent between devices are 32-bit elements; how exact they have to be, the bound alone decides.
A program may use at most 128 MiB of HBM per device.

v0:
```python
import math

import jax
import jax.numpy as jnp
from jax import lax
from jax.sharding import PartitionSpec as P

D = 5120
FF = 13824


DECAY = 0.95
LEARN_RATE = 0.02
EPSILON = 1e-08


def exact_dot(first, second):
    return jnp.dot(first, second, precision=lax.Precision.HIGHEST)


def make_basis(left_factor, gram_matrix):
    lower_factor = jnp.linalg.cholesky(gram_matrix)
    identity = jnp.eye(gram_matrix.shape[0], dtype=jnp.float32)
    inverse = lax.linalg.triangular_solve(lower_factor, identity, left_side=True, lower=True)
    return exact_dot(left_factor, inverse.T)


def local(
    out_momentum,
    out_gradient,
    out_weight,
    out_right,
    up_momentum,
    up_gradient,
    up_weight,
    up_right,
    down_momentum,
    down_gradient,
    down_weight,
    down_right,
):
    matrices = [
        (out_momentum, out_gradient, out_weight, out_right, D, D),
        (up_momentum, up_gradient, up_weight, up_right, D, FF),
        (down_momentum, down_gradient, down_weight, down_right, FF, D),
    ]
    buffers = [matrix[0] + matrix[1].astype(jnp.float32) for matrix in matrices]
    partial_left = [exact_dot(buffers[number], matrices[number][3]) for number in range(3)]
    left_factors = []
    grams = []
    for partial_value in partial_left:
        left_factor = lax.psum(partial_value, "tp")
        left_factors.append(left_factor)
        grams.append(lax.psum(exact_dot(left_factor.T, left_factor), ("fsdp", "rep")))
    moments = []
    weights = []
    factors = []
    changes = []
    for number in range(3):
        buffer = buffers[number]
        weight = matrices[number][2]
        row_total = matrices[number][4]
        col_total = matrices[number][5]
        left_basis = make_basis(left_factors[number], grams[number])
        summed_factor = lax.psum(exact_dot(buffer.T, left_basis), ("fsdp", "rep"))
        column_squares = lax.psum(jnp.sum(summed_factor * summed_factor, axis=0), "tp")
        moments.append(buffer - (1.0 - DECAY) * exact_dot(left_basis, summed_factor.T))
        right_next = summed_factor / (jnp.sqrt(column_squares) + EPSILON)
        factors.append(right_next)
        step_size = LEARN_RATE * math.sqrt(row_total / col_total)
        change = step_size * exact_dot(left_basis, right_next.T)
        changes.append(change)
        weights.append((weight.astype(jnp.float32) - change).astype(jnp.bfloat16))
    return (
        moments[0],
        moments[1],
        moments[2],
        weights[0],
        weights[1],
        weights[2],
        factors[0],
        factors[1],
        factors[2],
        changes[0],
        changes[1],
        changes[2],
    )


def solution(mesh):
    in_specs = (
        P(("fsdp", "rep"), "tp"),
        P(("fsdp", "rep"), "tp"),
        P(("fsdp", "rep"), "tp"),
        P("tp", None),
        P(("fsdp", "rep"), "tp"),
        P(("fsdp", "rep"), "tp"),
        P(("fsdp", "rep"), "tp"),
        P("tp", None),
        P(("fsdp", "rep"), "tp"),
        P(("fsdp", "rep"), "tp"),
        P(("fsdp", "rep"), "tp"),
        P("tp", None),
    )
    out_specs = (
        P(("fsdp", "rep"), "tp"),
        P(("fsdp", "rep"), "tp"),
        P(("fsdp", "rep"), "tp"),
        P(("fsdp", "rep"), "tp"),
        P(("fsdp", "rep"), "tp"),
        P(("fsdp", "rep"), "tp"),
        P("tp", None),
        P("tp", None),
        P("tp", None),
        P(("fsdp", "rep"), "tp"),
        P(("fsdp", "rep"), "tp"),
        P(("fsdp", "rep"), "tp"),
    )
    return jax.shard_map(local, mesh=mesh, in_specs=in_specs, out_specs=out_specs, check_vma=False)
```

profile of v0, /device:TPU:0, one launch (start us, length us, event | category | flops | bytes accessed | tf_op | source)
XLA Modules:
  0.0 511.9 jit_solution(8463808557629825897)
XLA Ops:
  7.3 3.5 fusion.8
  10.8 4.7 fusion.4
  15.5 5.0 fusion.6
  20.6 20.9 %all-reduce.15.cloned.1.call-done = (f32[80,128]{1,0:T(8,128)}, f32[80,128]{1,0:T(8,128)}) async-done(((f32[80,128]{1,0:T(8,128)}, f32[80,128]{1,0:T(8,128)}), (f32[80,128]{1,0:T(8,128)}, f32[80,128]{1,0:T(8,128)})) %all-reduce.15.cloned.1.call-update) | async-done | bytes 81936 | tf_op jit(solution)/shard_map/psum | solution.py:52
  45.0 24.2 %all-reduce.9.cloned.1.call-done = f32[216,128]{1,0:T(8,128)} async-done(((f32[216,128]{1,0:T(8,128)}), f32[216,128]{1,0:T(8,128)}) %all-reduce.9.cloned.1.call-update) | async-done | bytes 110608 | tf_op jit(solution)/shard_map/psum | solution.py:52
  71.8 130.9 %all-reduce.13.cloned.1.call-done = (f32[128,128]{0,1:T(8,128)}, f32[128,128]{0,1:T(8,128)}, f32[128,128]{0,1:T(8,128)}) async-done(((f32[128,128]{0,1:T(8,128)}, f32[128,128]{0,1:T(8,128)}, f32[128,128]{0,1:T(8,128)}), (f32[128,128]{0,1:T(8,128)}, f32[128,128]{0,1:T(8,128)}, f32[128,128]{0,1:T(8,128)})) %all-reduce.13.cloned.1.call-update) | async-done | bytes 196624 | tf_op jit(solution)/shard_map/psum | solution.py:54
  205.8 13.2 %cholesky.59 = f32[128,128]{1,0:T(8,128)} custom-call(f32[128,128]{1,0:T(8,128)} %fusion.23), custom_call_target="Cholesky" | custom-call | tf_op jit(solution)/shard_map/jit(cholesky)/cholesky | solution.py:22
  222.6 11.3 %custom-call.7 = f32[1,128,128]{1,2,0:T(8,128)} custom-call(f32[1,128,128]{2,1,0:T(8,128)} %fusion.15), custom_call_target="InvertDiagBlocksLowerTriangular" | custom-call | tf_op jit(solution)/shard_map/triangular_solve/custom-call.0 | solution.py:24
  241.4 13.2 %cholesky.81 = f32[128,128]{1,0:T(8,128)} custom-call(f32[128,128]{1,0:T(8,128)} %get-tuple-element.31), custom_call_target="Cholesky" | custom-call | tf_op jit(solution)/shard_map/jit(cholesky)/cholesky | solution.py:22
  256.1 2.1 fusion.17
  258.2 11.4 %custom-call.9 = f32[1,128,128]{1,2,0:T(8,128)} custom-call(f32[1,128,128]{2,1,0:T(8,128)} %fusion.17), custom_call_target="InvertDiagBlocksLowerTriangular" | custom-call | tf_op jit(solution)/shard_map/triangular_solve/custom-call.0 | solution.py:24
  271.4 13.2 %cholesky.70 = f32[128,128]{1,0:T(8,128)} custom-call(f32[128,128]{1,0:T(8,128)} %get-tuple-element.32), custom_call_target="Cholesky" | custom-call | tf_op jit(solution)/shard_map/jit(cholesky)/cholesky | solution.py:22
  288.2 11.3 %custom-call.8 = f32[1,128,128]{1,2,0:T(8,128)} custom-call(f32[1,128,128]{2,1,0:T(8,128)} %fusion.16), custom_call_target="InvertDiagBlocksLowerTriangular" | custom-call | tf_op jit(solution)/shard_map/triangular_solve/custom-call.0 | solution.py:24
  303.0 7.4 %fusion.5 = f32[2560,128]{1,0:T(8,128)} fusion(f32[216,128]{1,0:T(8,128)S(1)} %fusion.29, f32[216,2560]{1,0:T(8,128)} %param.23, bf16[216,2560]{1,0:T(8,128)(2,1)} %param.24), kind=kOutput, calls=%fused_computation.19 | convolution fusion | flops 850452480 | bytes 4739072 | tf_op jit(solution)/shard_map/dot_general | solution.py:18
  310.4 3.5 fusion.7
  313.9 7.5 %fusion.3 = f32[6912,128]{1,0:T(8,128)} fusion(f32[80,128]{1,0:T(8,128)S(1)} %fusion.27, f32[80,6912]{1,0:T(8,128)S(1)} %copy-done.5, bf16[80,6912]{1,0:T(8,128)(2,1)S(1)} %copy-done.12), kind=kOutput, calls=%fused_computation.17 | convolution fusion | flops 850452480 | bytes 6897664 | tf_op jit(solution)/shard_map/dot_general | solution.py:18
  321.4 145.2 %all-reduce.11.cloned.1.call-done = (f32[2560,128]{1,0:T(8,128)}, f32[6912,128]{1,0:T(8,128)}, f32[2560,128]{1,0:T(8,128)}) async-done(((f32[2560,128]{1,0:T(8,128)}, f32[6912,128]{1,0:T(8,128)}, f32[2560,128]{1,0:T(8,128)}), (f32[2560,128]{1,0:T(8,128)}, f32[6912,128]{1,0:T(8,128)}, f32[2560,128]{1,0:T(8,128)})) %all-reduce.11.cloned.1.call-update) | async-done | bytes 6160400 | tf_op jit(solution)/shard_map/psum | solution.py:65
  468.5 3.8 fusion.2
  472.7 4.6 fusion.1
  479.3 5.5 %fusion = f32[80,6912]{1,0:T(8,128)} fusion(f32[80,128]{1,0:T(8,128)S(1)} %copy-done.25, f32[6912,128]{1,0:T(8,128)S(1)} %copy-done.1, f32[80,6912]{1,0:T(8,128)S(1)} %copy-done.6, bf16[80,6912]{1,0:T(8,128)(2,1)S(1)} %copy-done.13), kind=kOutput, calls=%fused_computation.2 | convolution fusion | flops 851558400 | bytes 9109504 | tf_op jit(solution)/shard_map/dot_general | solution.py:18
  484.8 3.0 all-reduce.2
  492.9 2.6 subtract_convert_fusion.2
  495.5 3.8 subtract_convert_fusion
  499.4 5.6 %subtract_convert_fusion.1 = (bf16[80,6912]{1,0:T(8,128)(2,1)}, f32[80,6912]{1,0:T(8,128)}) fusion(bf16[80,6912]{1,0:T(8,128)(2,1)S(1)} %copy-done.21, f32[80,128]{1,0:T(8,128)S(1)} %copy-done.26, f32[6912,128]{1,0:T(8,128)S(1)} %broadcast_divide_fusion), kind=kOutput, calls=%fused_computation.11 | convolution fusion | flops 851558400 | bytes 8003584 | tf_op jit(solution)/shard_map/dot_general | solution.py:18
  (95 shorter events, 40.1 us)
Async XLA Ops:
  7.2 3.6 copy-start
  7.2 34.3 %all-reduce.15.cloned.1.call-start = ((), (), s32[]{:S(2)}) async-start(), calls=%async_computation.3 | async-start | bytes 163840 | tf_op jit(solution)/shard_map/psum | solution.py:52
  7.2 3.5 copy-start.4
  15.5 53.8 %all-reduce.9.cloned.1.call-start = ((), (), s32[]{:S(2)}) async-start(), calls=%async_computation | async-start | bytes 221184 | tf_op jit(solution)/shard_map/psum | solution.py:52
  20.5 182.2 %all-reduce.13.cloned.1.call-start = ((), (), s32[]{:S(2)}) async-start(), calls=%async_computation.2 | async-start | bytes 393216 | tf_op jit(solution)/shard_map/psum | solution.py:54
  71.3 395.4 %all-reduce.11.cloned.1.call-start = ((), (), s32[]{:S(2)}) async-start(), calls=%async_computation.1 | async-start | bytes 12320768 | tf_op jit(solution)/shard_map/psum | solution.py:65
  301.7 12.2 %copy-start.24 = (f32[80,128]{1,0:T(8,128)}, f32[80,128]{1,0:T(8,128)S(1)}, u32[]{:S(2)}) copy-start(f32[80,128]{1,0:T(8,128)S(1)} %fusion.27) | copy-start | bytes 122884
  303.0 7.4 %copy-start.18 = (f32[216,128]{1,0:T(8,128)}, f32[216,128]{1,0:T(8,128)S(1)}, u32[]{:S(2)}) copy-start(f32[216,128]{1,0:T(8,128)S(1)} %fusion.29) | copy-start | bytes 331780
  303.0 7.4 %copy-start.14 = (f32[80,2560]{1,0:T(8,128)S(1)}, f32[80,2560]{1,0:T(8,128)}, u32[]{:S(2)}) copy-start(f32[80,2560]{1,0:T(8,128)} %param.15) | copy-start | bytes 2457604
  303.0 7.4 %copy-start.17 = (bf16[80,2560]{1,0:T(8,128)(2,1)S(1)}, bf16[80,2560]{1,0:T(8,128)(2,1)}, u32[]{:S(2)}) copy-start(bf16[80,2560]{1,0:T(8,128)(2,1)} %param.16) | copy-start | bytes 1228804
  303.0 7.4 %copy-start.22 = (f32[80,128]{1,0:T(8,128)S(1)}, f32[80,128]{1,0:T(8,128)}, u32[]{:S(2)}) copy-start(f32[80,128]{1,0:T(8,128)} %fusion.25) | copy-start | bytes 122884
  303.0 10.9 %copy-start.12 = (bf16[80,6912]{1,0:T(8,128)(2,1)S(1)}, bf16[80,6912]{1,0:T(8,128)(2,1)}, u32[]{:S(2)}) copy-start(bf16[80,6912]{1,0:T(8,128)(2,1)} %param.20) | copy-start | bytes 3317764
  310.4 3.5 copy-start.5
  466.7 5.7 %copy-start.9 = (f32[2560,128]{1,0:T(8,128)S(1)}, f32[2560,128]{1,0:T(8,128)}, u32[]{:S(2)}) copy-start(f32[2560,128]{1,0:T(8,128)} %get-tuple-element.16) | copy-start | bytes 3932164
  468.5 4.2 copy-start.3
  468.5 4.2 copy-start.11
  472.7 4.6 copy-start.1
  487.7 3.0 copy-start.10
  491.6 3.9 copy-start.16
  492.9 6.4 %copy-start.7 = (f32[6912,128]{1,0:T(8,128)}, f32[6912,128]{1,0:T(8,128)S(1)}, u32[]{:S(2)}) copy-start(f32[6912,128]{1,0:T(8,128)S(1)} %broadcast_divide_fusion) | copy-start | bytes 10616836
  492.9 2.6 copy-start.19
  492.9 2.6 copy-start.20
  495.5 3.8 copy-start.21
  495.5 3.8 copy-start.26
  (8 other events, 12.8 us)
Sparse Core Ops, SparseCore 0:
  15.6 25.8 all-reduce.14
  44.4 24.7 all-reduce.8
  75.4 127.2 all-reduce.12
  321.6 145.0 all-reduce.10
where the time goes:
time: 520 us; the launch traced here: 512 us
  waiting for transfers between devices  321 us (62%)
  other arithmetic  94 us (18%)
  matrix products  71 us (14%)
  between operations  14.5 us (3%)
  local copies, waits for them, and re-layouts  7.59 us (1%)
    psum x1, waiting for transfers between devices, local(): summed_factor = lax.psum(exact_dot(buffer.T, left_basis), ('fsdp', 'rep'))  145 us
    psum x1, waiting for transfers between devices, local(): lax.psum(exact_dot(left_factor.T, left_factor), ('fsdp', 'rep'))  131 us
    dot_general x18, matrix products, exact_dot(): return jnp.dot(first, second, precision=lax.Precision.HIGHEST)  67 us
    psum x2, waiting for transfers between devices, local(): left_factor = lax.psum(partial_value, 'tp')  45.1 us
    another operation x9, other arithmetic, make_basis(): lower_factor = jnp.linalg.cholesky(gram_matrix)  44.1 us
    another operation x6, other arithmetic, make_basis(): lax.linalg.triangular_solve(lower_factor, identity, left_side=True, lower...  40.4 us
  transfers between devices with their start and end apart: 4, of which 4 were waited for; matrix products, arithmetic and copies ran while one was open for 2% of the time, Pallas kernels for 0%

commit v1 on v0

v1 whole, which is shorter than its diff:
```python
import functools
import math

import jax
import jax.numpy as jnp
from jax import lax
from jax.experimental import pallas as pl
from jax.experimental.pallas import tpu as pltpu
from jax.sharding import PartitionSpec as P

ROWS = (216, 80, 80)
PADDED = (224, 80, 80)
COLS = (2560, 2560, 6912)
UNITS = (5, 5, 14)
SPANS = ((1280, 1280), (1280, 1280), (2304, 2304, 2304))
SHAPE = ((13824, 5120), (5120, 5120), (5120, 13824))
UNIT = 512
RANK = 128
DECAY = 0.95
LEARN_RATE = 0.02
EPSILON = 1e-08
MESH = pl.DeviceIdType.MESH
F32 = jnp.float32
BF16 = jnp.bfloat16
HIGHEST = lax.Precision.HIGHEST
AXES = ((0, 1, 2), (1, 2, 0), (2, 0, 1))
TERMS = tuple(3 * rows + (-3 * rows) % 128 for rows in PADDED)

PER_PART = (3, 5)


def make_parts():
    units = [(matrix, unit) for matrix in range(3) for unit in range(UNITS[matrix])]
    parts = []
    for count in PER_PART:
        for _ in range(3):
            parts.append(units[:count])
            units = units[count:]
    return parts


PARTS = make_parts()
N_PARTS = len(PARTS)
HEIGHT = [8 * len(part) for part in PARTS]


def split(value):
    high = value.astype(BF16)
    return high, (value - high.astype(F32)).astype(BF16)


def nt_dot(first, second, precision=None):
    return lax.dot_general(first, second, (((1,), (1,)), ((), ())), precision=precision, preferred_element_type=F32)


def tn_dot(first, second, precision=None):
    return lax.dot_general(first, second, (((0,), (0,)), ((), ())), precision=precision, preferred_element_type=F32)


def each(count, body):
    def step(index, carry):
        body(index)
        return carry

    lax.fori_loop(0, count, step, 0)


def reduce_kernel(
    momentum,
    gradient,
    right,
    factor,
    buffer,
    basis,
    squares,
    partial,
    summed,
    inbox1,
    inbox2,
    inbox3,
    grad_in,
    right_in,
    terms,
    right_terms,
    left,
    left_in,
    left_terms,
    gram,
    gram_in1,
    gram_in2,
    gram_in3,
    gram_sum,
    gram_all,
    matrix,
    inverse,
    squares_in,
    load_sem,
    send_sem,
    recv_sem,
    misc_send,
    misc_recv,
):
    rows_at = lax.axis_index("fsdp")
    core = lax.axis_index("tp")
    coord = (lax.axis_index("rep"), rows_at % 4, rows_at // 4)

    def device(axis, shift):
        moved = [(coord[a] + shift) % 4 if a == axis else coord[a] for a in range(3)]
        return (moved[2] * 4 + moved[1], core, moved[0])

    partner = (rows_at, 1 - core, coord[0])

    loads = []
    for j in range(3):
        steps = []
        start = 0
        for s, span in enumerate(SPANS[j]):
            cols = pl.ds(start, span)
            copies = [
                pltpu.make_async_copy(momentum[j].at[:, cols], buffer[j].at[:, cols], load_sem.at[j, s, 0]),
                pltpu.make_async_copy(gradient[j].at[:, cols], grad_in[j].at[:, cols], load_sem.at[j, s, 1]),
                pltpu.make_async_copy(right[j].at[cols, :], right_in[j].at[cols, :], load_sem.at[j, s, 2]),
            ]
            for copy in copies:
                copy.start()
            steps.append((start, span, copies))
            start += span
        loads.append(steps)

    barrier = pltpu.get_barrier_semaphore()
    peers = [device(axis, shift) for axis in range(3) for shift in (1, 2, 3)] + [partner]
    for peer in peers:
        pl.semaphore_signal(barrier, inc=1, device_id=peer, device_id_type=MESH)

    started = []

    def send(index, src, dst, target, sems=None):
        first, second = (send_sem, recv_sem) if sems is None else sems
        copy = pltpu.make_async_remote_copy(
            src_ref=src,
            dst_ref=dst,
            send_sem=first.at[index],
            recv_sem=second.at[index],
            device_id=target,
            device_id_type=MESH,
        )
        copy.start()
        started.append(copy)
        return copy

    misc = functools.partial(send, sems=(misc_send, misc_recv))

    def left_partial(j):
        pad = PADDED[j]
        total = None
        for start, span, copies in loads[j]:
            for copy in copies:
                copy.wait()

            def prepare(i, start=start):
                cols = pl.ds(pl.multiple_of(start + i * 256, 256), 256)
                value = buffer[j][:, cols] + grad_in[j][:, cols].astype(F32)
                buffer[j][:, cols] = value
                if pad > ROWS[j]:
                    value = jnp.concatenate([value, jnp.zeros((pad - ROWS[j], 256), F32)], axis=0)
                high, low = split(value)
                terms[j][0:pad, cols] = high
                terms[j][pad : 2 * pad, cols] = low
                terms[j][2 * pad : 3 * pad, cols] = high
                high, low = split(right_in[j][cols, :])
                right_terms[j][cols, 0:RANK] = high
                right_terms[j][cols, RANK : 2 * RANK] = low

            each(span // 256, prepare)
            product = jnp.dot(
                terms[j][0 : 2 * pad, start : start + span],
                right_terms[j][start : start + span, :],
                preferred_element_type=F32,
            )
            product = product[0:pad, 0:RANK] + (product[0:pad, RANK:] + product[pad:, 0:RANK])
            total = product if total is None else total + product
        left[j][...] = total
        if terms[j].shape[1] > COLS[j]:
            terms[j][:, COLS[j] :] = jnp.zeros((3 * pad, terms[j].shape[1] - COLS[j]), BF16)
        return misc(j, left[j], left_in[j], partner)

    def left_finish(j, copy):
        copy.wait_recv()
        pad = PADDED[j]
        value = left[j][...] + left_in[j][...]
        left_in[j][...] = value
        high = value.astype(BF16).astype(F32)
        low = value - high
        pieces = [high, high, low]
        if TERMS[j] > 3 * pad:
            pieces.append(jnp.zeros((TERMS[j] - 3 * pad, RANK), F32))
        left_terms[j][...] = jnp.concatenate(pieces, axis=0).T.astype(BF16)

    def gram_partial(j):
        value = left_in[j][...]
        result = tn_dot(value, value, HIGHEST)
        gram[:, :, j] = result.reshape(2, 4, 16, RANK)

    def factor_unit(k, slot):
        j, unit = PARTS[k][slot]
        cols = slice(unit * UNIT, (unit + 1) * UNIT)
        product = jnp.dot(left_terms[j][:, 0 : 3 * PADDED[j]], terms[j][:, cols], preferred_element_type=F32)
        partial[k][:, slot * 8 : slot * 8 + 8, :] = product.T.reshape(64, 8, RANK)

    def factor_part(k):
        for slot in range(len(PARTS[k])):
            factor_unit(k, slot)

    def place(ref, base, half, chunk, side):
        return ref.at[pl.ds(base + ((chunk % 4) * 2 + side) * half, half)]

    def setting(k, phase):
        axes = AXES[k % 3]
        first = coord[axes[0]]
        axis = axes[phase - 1]
        return axis, coord[axis], 16 * first

    def reduce_start(k, phase):
        axis, i, base = setting(k, phase)
        base, half, inbox = (0, 8, inbox1[k]) if phase == 1 else (base, 2, inbox2[k])
        at = functools.partial(place, partial[k], base, half)
        n = 0 if phase == 1 else 6
        up, down = device(axis, 1), device(axis, 3)
        return [
            send((k, n), at(i + 2, 0), inbox.at[0], up),
            send((k, n + 1), at(i + 2, 1), inbox.at[1], down),
            send((k, n + 2), at(i + 1, 1), inbox.at[2], up),
            send((k, n + 3), at(i + 3, 0), inbox.at[3], down),
        ]

    def reduce_relay(k, phase, copies):
        axis, i, base = setting(k, phase)
        base, half, inbox = (0, 8, inbox1[k]) if phase == 1 else (base, 2, inbox2[k])
        n = 0 if phase == 1 else 6
        for source, chunk, shift in ((0, i + 1, 1), (1, i + 3, 3)):
            copies[source].wait_recv()
            ref = place(partial[k], base, half, chunk, source)

            def add(s, ref=ref, source=source):
                ref[s] += inbox[source, s]

            each(half, add)
            copies.append(send((k, n + 4 + source), ref, inbox.at[4 + source], device(axis, shift)))

    def reduce_finish(k, phase, copies):
        axis, i, base = setting(k, phase)
        base, half, inbox = (0, 8, inbox1[k]) if phase == 1 else (base, 2, inbox2[k])
        for n in (2, 3, 4, 5):
            copies[n].wait_recv()
        for side, near, relayed in ((0, 3, 4), (1, 2, 5)):
            ref = place(partial[k], base, half, i, side)

            def add(s, ref=ref, near=near, relayed=relayed):
                ref[s] += inbox[near, s] + inbox[relayed, s]

            each(half, add)

    def own(k):
        axes = AXES[k % 3]
        return 4 * coord[axes[1]] + coord[axes[2]]

    def last_reduce_start(k):
        axis, i, base = setting(k, 3)
        base = base + 4 * coord[AXES[k % 3][1]]
        return [
            send((k, 11 + s), partial[k].at[base + (i + s) % 4], inbox3[k].at[s - 1], device(axis, s))
            for s in (1, 2, 3)
        ]

    def last_reduce_finish(k, copies):
        for copy in copies:
            copy.wait_recv()
        mine = partial[k][16 * coord[AXES[k % 3][0]] + own(k)]
        summed[k][own(k)] = (mine + inbox3[k][0]) + (inbox3[k][1] + inbox3[k][2])

    def first_gather_start(k):
        axis, _, _ = setting(k, 3)
        ref = summed[k].at[own(k)]
        return [send((k, 14 + s), ref, ref, device(axis, s)) for s in (1, 2, 3)]

    def gather_start(k, phase):
        axis, i, _ = setting(k, phase)
        ref, half, n = (factor[k], 8, 24) if phase == 1 else (summed[k], 2, 18)
        at = functools.partial(place, ref, 0, half)
        up, down = device(axis, 1), device(axis, 3)
        return [
            send((k, n), at(i, 0), at(i, 0), up),
            send((k, n + 1), at(i, 1), at(i, 1), down),
            send((k, n + 2), at(i, 1), at(i, 1), up),
            send((k, n + 3), at(i, 0), at(i, 0), down),
        ]

    def gather_relay(k, phase, copies):
        axis, i, _ = setting(k, phase)
        ref, half, n = (factor[k], 8, 24) if phase == 1 else (summed[k], 2, 18)
        at = functools.partial(place, ref, 0, half)
        copies[0].wait_recv()
        copies.append(send((k, n + 4), at(i + 3, 0), at(i + 3, 0), device(axis, 1)))
        copies[1].wait_recv()
        copies.append(send((k, n + 5), at(i + 1, 1), at(i + 1, 1), device(axis, 3)))

    def gather_finish(k, copies):
        for n in (2, 3, 4, 5):
            copies[n].wait_recv()

    def apply_inverse(k):
        base = 16 * coord[AXES[k % 3][0]]
        for slot, (j, _) in enumerate(PARTS[k]):
            rows = slice(slot * 8, slot * 8 + 8)
            value = summed[k][:, rows, :].reshape(128, RANK)
            factor[k][pl.ds(base, 16), rows, :] = nt_dot(value, inverse[j], HIGHEST).reshape(16, 8, RANK)

    def gram_scatter():
        x = coord[0]
        return [
            misc(2 + s, gram.at[core, (x + s) % 4], gram_in1.at[x], device(0, s)) for s in (1, 2, 3)
        ]

    def gram_exchange(copies, own_value, box, sent, axis, n):
        for copy in copies:
            copy.wait_recv()
        box_before, at_before = own_value
        box_before[at_before] = sent[0][...]
        sent[1][...] = (box_before[0] + box_before[1]) + (box_before[2] + box_before[3])
        return [misc(n + s, sent[1], box.at[coord[axis]], device(axis, s)) for s in (1, 2, 3)]

    def gram_gather(copies):
        x = coord[0]
        for copy in copies:
            copy.wait_recv()
        gram_in3[coord[2]] = gram_sum[1]
        ref = gram_all.at[core, x]
        ref[...] = (gram_in3[0] + gram_in3[1]) + (gram_in3[2] + gram_in3[3])
        return [misc(11 + s, ref, ref, device(0, s)) for s in (1, 2, 3)]

    def gram_swap(copies):
        for copy in copies:
            copy.wait_recv()
        return misc(15, gram_all.at[core], gram_all.at[core], partner)

    lane = lax.broadcasted_iota(jnp.int32, (8, RANK), 1)
    sublane = lax.broadcasted_iota(jnp.int32, (8, RANK), 0)

    def gram_finish(copy):
        copy.wait_recv()
        row = lax.broadcasted_iota(jnp.int32, (RANK, RANK), 0)
        col = lax.broadcasted_iota(jnp.int32, (RANK, RANK), 1)
        for j in range(3):
            matrix[j, :, 0:RANK] = gram_all[:, :, j].reshape(RANK, RANK)
            matrix[j, :, RANK:] = (row == col).astype(F32)

    def eliminate(block):
        first = pl.multiple_of(block * 8, 8)
        panels = []
        for j in range(3):
            both = matrix[j, pl.ds(first, 8), :]
            panels.append([pltpu.roll(both[:, 0:RANK], (RANK - first) % RANK, 1), both[:, RANK:]])
        for step in range(8):
            for j in range(3):
                a, x = panels[j]
                pivot = jnp.broadcast_to(a[step : step + 1, step : step + 1], (8, RANK))
                scale = 1.0 / jnp.sqrt(pivot)
                column = jnp.broadcast_to(a[:, step : step + 1], (8, RANK)) * scale
                column = jnp.where(sublane > step, column, 0.0)
                row_a = jnp.broadcast_to(a[step : step + 1, :], (8, RANK)) * scale
                row_x = jnp.broadcast_to(x[step : step + 1, :], (8, RANK)) * scale
                here = sublane == step
                panels[j] = [
                    jnp.where(here, row_a, a - column * row_a),
                    jnp.where(here, row_x, x - column * row_x),
                ]
        for j in range(3):
            a, x = panels[j]
            a = pltpu.roll(a, first, 1)
            a = jnp.where(lane >= first + 8, a, 0.0)
            inverse[j, pl.ds(first, 8), :] = x
            matrix[j] = matrix[j] - tn_dot(a, jnp.concatenate([a, x], axis=1), HIGHEST)

    def eliminate_blocks(start, stop):
        def step(block, carry):
            eliminate(block)
            return carry

        lax.fori_loop(start, stop, step, 0)

    wave0 = (0, 1, 2)
    wave1 = (3, 4, 5)
    flying = {}

    pl.semaphore_wait(barrier, len(peers))
    left_copies = [left_partial(0), left_partial(1)]
    left_finish(0, left_copies[0])
    factor_part(0)
    flying[0] = reduce_start(0, 1)
    left_finish(1, left_copies[1])
    for k in (1, 2):
        factor_part(k)
        flying[k] = reduce_start(k, 1)
    left_copies.append(left_partial(2))
    for j in (0, 1):
        gram_partial(j)
    left_finish(2, left_copies[2])
    gram_partial(2)
    gram_copies = gram_scatter()
    for k in wave0:
        reduce_relay(k, 1, flying[k])
    for k in wave1:
        factor_part(k)
        flying[k] = reduce_start(k, 1)
    gram_copies = gram_exchange(gram_copies, (gram_in1, coord[0]), gram_in2, (gram.at[core, coord[0]], gram_sum.at[0]), 1, 5)
    for k in wave0:
        reduce_finish(k, 1, flying[k])
        flying[k] = reduce_start(k, 2)
    gram_copies = gram_exchange(gram_copies, (gram_in2, coord[1]), gram_in3, (gram_sum.at[0], gram_sum.at[1]), 2, 8)
    for k in wave0:
        reduce_relay(k, 2, flying[k])
    for k in wave1:
        reduce_relay(k, 1, flying[k])
    gram_copies = gram_gather(gram_copies)
    for k in wave0:
        reduce_finish(k, 2, flying[k])
        flying[k] = last_reduce_start(k)
    gram_copy = gram_swap(gram_copies)
    gram_finish(gram_copy)
    eliminate_blocks(0, 4)
    for k in wave0:
        last_reduce_finish(k, flying[k])
        flying[k] = first_gather_start(k)
    for k in wave1:
        reduce_finish(k, 1, flying[k])
        flying[k] = reduce_start(k, 2)
    eliminate_blocks(4, 7)
    for k in wave0:
        gather_finish_direct(flying[k])
        flying[k] = gather_start(k, 2)
    for k in wave1:
        reduce_relay(k, 2, flying[k])
    eliminate_blocks(7, 10)
    for k in wave0:
        gather_relay(k, 2, flying[k])
    for k in wave1:
        reduce_finish(k, 2, flying[k])
        flying[k] = last_reduce_start(k)
    eliminate_blocks(10, 16)
    for k in wave0:
        gather_finish(k, flying[k])
        apply_inverse(k)
        flying[k] = gather_start(k, 1)
    for k in wave1:
        last_reduce_finish(k, flying[k])
        flying[k] = first_gather_start(k)
    for j in range(3):
        basis[j][...] = nt_dot(left_in[j][...], inverse[j], HIGHEST)[0 : ROWS[j]]
    for k in wave1:
        gather_finish_direct(flying[k])
        flying[k] = gather_start(k, 2)
    for k in wave0:
        gather_relay(k, 1, flying[k])
    for k in wave1:
        gather_relay(k, 2, flying[k])
    for k in wave1:
        gather_finish(k, flying[k])
        apply_inverse(k)
        flying[k] = gather_start(k, 1)
    for k in wave0:
        gather_finish(k, flying[k])
    sums = [jnp.zeros((8, RANK), F32) for _ in range(3)]

    def add_squares(k, sums):
        for slot, (j, _) in enumerate(PARTS[k]):
            def step(i, total, slot=slot):
                value = factor[k][pl.ds(i * 8, 8), slot * 8 : slot * 8 + 8, :]
                return total + jnp.sum(value * value, axis=0)

            sums[j] = lax.fori_loop(0, 8, step, sums[j])

    for k in wave0:
        add_squares(k, sums)
    for k in wave1:
        gather_relay(k, 1, flying[k])
    for k in wave1:
        gather_finish(k, flying[k])
        add_squares(k, sums)
    rows = [jnp.sum(value, axis=0, keepdims=True) for value in sums]
    squares_in[0] = jnp.concatenate(rows + [jnp.zeros((5, RANK), F32)], axis=0)
    copy = misc(16, squares_in.at[0], squares_in.at[1], partner)
    copy.wait_recv()
    squares[...] = squares_in[0] + squares_in[1]
    for copy in started:
        copy.wait_send()


def gather_finish_direct(copies):
    for copy in copies:
        copy.wait_recv()


def update_kernel(
    weight,
    factor,
    buffer,
    basis,
    squares,
    moment_out,
    weight_out,
    right_out,
    change_out,
    weight_in,
    moment_box,
    weight_box,
    right_box,
    change_box,
    rows_in,
    load_sem,
    store_sem,
):
    loads = [pltpu.make_async_copy(weight[j], weight_in[j], load_sem.at[j]) for j in range(3)]
    for copy in loads:
        copy.start()
    scale = 1.0 / (jnp.sqrt(squares[...]) + EPSILON)
    for j in range(3):
        rows, pad = ROWS[j], PADDED[j]
        value = basis[j][...]
        if pad > rows:
            value = jnp.concatenate([value, jnp.zeros((pad - rows, RANK), F32)], axis=0)
        step_size = LEARN_RATE * math.sqrt(SHAPE[j][0] / SHAPE[j][1])
        high, low = split(value * (scale[j : j + 1] * step_size))
        rows_in[j][0:pad, 0:RANK] = high
        rows_in[j][0:pad, RANK:] = high
        rows_in[j][pad : 2 * pad, 0:RANK] = low
        rows_in[j][pad : 2 * pad, RANK:] = jnp.zeros((pad, RANK), BF16)
        moment = (value * (1.0 - DECAY)).astype(BF16)
        rows_in[j][2 * pad :, 0:RANK] = moment
        rows_in[j][2 * pad :, RANK:] = jnp.zeros((pad, RANK), BF16)
    waited = [False] * 3
    stores = []
    for k in range(N_PARTS):
        for slot, (j, unit) in enumerate(PARTS[k]):
            if not waited[j]:
                loads[j].wait()
                waited[j] = True
            rows, pad = ROWS[j], PADDED[j]
            start = unit * UNIT
            width = min(UNIT, COLS[j] - start)
            value = factor[k][0 : width // 8, slot * 8 : slot * 8 + 8, :].reshape(width, RANK)
            cols = slice(start, start + width)
            right_box[j][cols, :] = value * scale[j : j + 1]
            high, low = split(value)
            product = nt_dot(rows_in[j][...], jnp.concatenate([high, low], axis=1))
            change = product[0:rows] + product[pad : pad + rows]
            change_box[j][:, cols] = change
            moment_box[j][:, cols] = buffer[j][:, cols] - product[2 * pad : 2 * pad + rows]
            weight_box[j][:, cols] = (weight_in[j][:, cols].astype(F32) - change).astype(BF16)
            pairs = (
                (right_box[j].at[cols, :], right_out[j].at[cols, :]),
                (change_box[j].at[:, cols], change_out[j].at[:, cols]),
                (moment_box[j].at[:, cols], moment_out[j].at[:, cols]),
                (weight_box[j].at[:, cols], weight_out[j].at[:, cols]),
            )
            for n, (src, dst) in enumerate(pairs):
                copy = pltpu.make_async_copy(src, dst, store_sem.at[k, slot, n])
                copy.start()
                stores.append(copy)
    for copy in stores:
        copy.wait()


def local(
    out_momentum,
    out_gradient,
    out_weight,
    out_right,
    up_momentum,
    up_gradient,
    up_weight,
    up_right,
    down_momentum,
    down_gradient,
    down_weight,
    down_right,
):
    momentum = [down_momentum, out_momentum, up_momentum]
    gradient = [down_gradient, out_gradient, up_gradient]
    weight = [down_weight, out_weight, up_weight]
    right = [down_right, out_right, up_right]
    vmem = pltpu.VMEM
    anywhere = pl.BlockSpec(memory_space=pl.ANY)
    inside = pl.BlockSpec(memory_space=vmem)
    dma = pltpu.SemaphoreType.DMA
    each_part = lambda lead: [vmem((*lead, HEIGHT[k], RANK), F32) for k in range(N_PARTS)]

    factor_shapes = [jax.ShapeDtypeStruct((64, HEIGHT[k], RANK), F32) for k in range(N_PARTS)]
    buffer_shapes = [jax.ShapeDtypeStruct((ROWS[j], COLS[j]), F32) for j in range(3)]
    basis_shapes = [jax.ShapeDtypeStruct((ROWS[j], RANK), F32) for j in range(3)]
    middle = [factor_shapes, buffer_shapes, basis_shapes, jax.ShapeDtypeStruct((8, RANK), F32)]
    placed = jax.tree.map(lambda s: vmem(s.shape, s.dtype), middle)
    terms_cols = [UNIT * count for count in UNITS]
    factor, buffer, basis, squares = pl.pallas_call(
        reduce_kernel,
        out_shape=placed,
        in_specs=[[anywhere] * 3] * 3,
        out_specs=jax.tree.map(lambda s: inside, middle),
        scratch_shapes=[
            each_part((64,)),
            each_part((16,)),
            each_part((6, 8)),
            each_part((6, 2)),
            each_part((3,)),
            [vmem((ROWS[j], COLS[j]), BF16) for j in range(3)],
            [vmem((COLS[j], RANK), F32) for j in range(3)],
            [vmem((3 * PADDED[j], terms_cols[j]), BF16) for j in range(3)],
            [vmem((COLS[j], 2 * RANK), BF16) for j in range(3)],
            [vmem((PADDED[j], RANK), F32) for j in range(3)],
            [vmem((PADDED[j], RANK), F32) for j in range(3)],
            [vmem((RANK, TERMS[j]), BF16) for j in range(3)],
            vmem((2, 4, 3, 16, RANK), F32),
            vmem((4, 3, 16, RANK), F32),
            vmem((4, 3, 16, RANK), F32),
            vmem((4, 3, 16, RANK), F32),
            vmem((2, 3, 16, RANK), F32),
            vmem((2, 4, 3, 16, RANK), F32),
            vmem((3, RANK, 2 * RANK), F32),
            vmem((3, RANK, RANK), F32),
            vmem((2, 8, RANK), F32),
            dma((3, 3, 3)),
            dma((N_PARTS, 30)),
            dma((N_PARTS, 30)),
            dma((17,)),
            dma((17,)),
        ],
        compiler_params=pltpu.CompilerParams(
            collective_id=0, has_side_effects=True, vmem_limit_bytes=50 * 2**20
        ),
        name="reduce",
    )(momentum, gradient, right)
    keep = lambda x: pltpu.with_memory_space_constraint(x, vmem)
    factor, buffer, basis, squares = jax.tree.map(keep, (factor, buffer, basis, squares))
    matrices = lambda dtype: [jax.ShapeDtypeStruct((ROWS[j], COLS[j]), dtype) for j in range(3)]
    factors = [jax.ShapeDtypeStruct((COLS[j], RANK), F32) for j in range(3)]
    results = [matrices(F32), matrices(BF16), factors, matrices(F32)]
    moment, weight, right, change = pl.pallas_call(
        update_kernel,
        out_shape=results,
        in_specs=[[anywhere] * 3, [inside] * N_PARTS, [inside] * 3, [inside] * 3, inside],
        out_specs=jax.tree.map(lambda s: anywhere, results),
        scratch_shapes=[
            [vmem((ROWS[j], COLS[j]), BF16) for j in range(3)],
            [vmem((ROWS[j], COLS[j]), F32) for j in range(3)],
            [vmem((ROWS[j], COLS[j]), BF16) for j in range(3)],
            [vmem((COLS[j], RANK), F32) for j in range(3)],
            [vmem((ROWS[j], COLS[j]), F32) for j in range(3)],
            [vmem((3 * PADDED[j], 2 * RANK), BF16) for j in range(3)],
            dma((3,)),
            dma((N_PARTS, max(PER_PART), 4)),
        ],
        compiler_params=pltpu.CompilerParams(vmem_limit_bytes=44 * 2**20),
        name="update",
    )(weight, factor, buffer, basis, squares)
    pick = lambda group: (group[1], group[2], group[0])
    return (*pick(moment), *pick(weight), *pick(right), *pick(change))


def solution(mesh):
    matrix, factor = P(("fsdp", "rep"), "tp"), P("tp", None)
    in_specs = (matrix, matrix, matrix, factor) * 3
    out_specs = (matrix,) * 6 + (factor,) * 3 + (matrix,) * 3
    return jax.shard_map(local, mesh=mesh, in_specs=in_specs, out_specs=out_specs, check_vma=False)
```

time: 520 us -> 115 us (0.22); the launches traced: 512 us -> 113 us
  waiting for transfers between devices: 321 us -> 0 us
  Pallas kernels: 0 us -> 112 us
  other arithmetic: 94 us -> 0 us
  matrix products: 71 us -> 0 us
  between operations: 14.5 us -> 0.82 us
  local copies, waits for them, and re-layouts: 7.59 us -> 0 us
    psum x4 -> x0, waiting for transfers between devices: 321 us -> none  [the longest x1 145 us: local(): summed_factor = lax.psum(exact_dot(buffer.T, left_basis), ('fsdp', 'rep'))]
    pallas_call x0 -> x2, Pallas kernels: none -> 112 us  [the longest x1 103 us: local(): pl.pallas_call(reduce_kernel, out_shape=placed, in_specs=[[anywhere] * 3]...]
    another operation x15 -> x0, other arithmetic: 84.4 us -> none  [the longest x9 44.1 us: make_basis(): lower_factor = jnp.linalg.cholesky(gram_matrix)]
    dot_general x18 -> x0, matrix products: 67 us -> none  [exact_dot(): return jnp.dot(first, second, precision=lax.Precision.HIGHEST)]
  transfers between devices with their start and end apart: 4 -> 0, of which waited for: 4 -> 0; matrix products, arithmetic and copies ran while one was open for 2% -> 0% of each run, Pallas kernels for 0% -> 0%
where the time goes in v1:
time: 115 us; the launch traced here: 113 us
  Pallas kernels  112 us (97%)
    pallas_call x1, Pallas kernels, local(): pl.pallas_call(reduce_kernel, out_shape=placed, in_specs=[[anywhere] * 3]...  103 us
    pallas_call x1, Pallas kernels, local(): pl.pallas_call(update_kernel, out_shape=results, in_specs=[[anywhere] * 3...  9.09 us

profile of v1, /device:TPU:0, one launch (start us, length us, event | category | flops | bytes accessed | tf_op | source)
XLA Modules:
  0.0 112.9 jit_solution(11855164611998109954)
XLA Ops:
  0.6 103.0 %reduce.1 = (f32[64,24,128]{2,1,0:T(8,128)S(1)}, f32[64,24,128]{2,1,0:T(8,128)S(1)}, f32[64,24,128]{2,1,0:T(8,128)S(1)}, f32[64,40,128]{2,1,0:T(8,128)S(1)}, f32...) custom-call(f32[216,2560]{1,0:T(8,128)} %momentum_0_.1, ...), custom_call_target="tpu_custom_call" | custom-call | tf_op jit(solution)/shard_map/reduce/pallas_call | solution.py:603
  103.7 9.1 %update.1 = (f32[216,2560]{1,0:T(8,128)}, f32[80,2560]{1,0:T(8,128)}, f32[80,6912]{1,0:T(8,128)}, bf16[216,2560]{1,0:T(8,128)(2,1)}, bf16[80,2560]{1,0:T(8,128)(...) custom-call(bf16[216,2560]{1,0:T(8,128)(2,1)} %weight_0_.1, ...), custom_call_target="tpu_custom_call" | custom-call | tf_op jit(solution)/shard_map/update/pallas_call | solution.py:646

commit v2 on v1

--- a/solution.py
+++ b/solution.py
@@ -41,6 +41,53 @@
 
 PARTS = make_parts()
 N_PARTS = len(PARTS)
+GROUPS = ((1, (0, 1)), (1, (2, 3)), (1, (4,)), (0, (0, 1)), (0, (2, 3)), (0, (4,))) + tuple(
+    (2, (unit, unit + 1)) for unit in range(0, 14, 2)
+)
+PLAN = (
+    ("left", 0),
+    ("left", 1),
+    ("finish", 0),
+    ("finish", 1),
+    ("R1a", 0),
+    ("left", 2),
+    ("finish", 2),
+    ("gram", 0),
+    ("R1b", 0),
+    ("gram", 1),
+    ("R1a", 1),
+    ("gram", 2),
+    ("R1c", 0),
+    ("gram", 3),
+    ("R2b", 0),
+    ("gram", 4),
+    ("R1b", 1),
+    ("gram", 5),
+    ("chol", 0),
+    ("R2c", 0),
+    ("chol", 1),
+    ("R1c", 1),
+    ("R3c", 0),
+    ("chol", 2),
+    ("R2b", 1),
+    ("chol", 3),
+    ("G3c", 0),
+    ("chol", 4),
+    ("R2c", 1),
+    ("G2b", 0),
+    ("chol", 5),
+    ("R3c", 1),
+    ("chol", 6),
+    ("chol", 7),
+    ("G2c", 0),
+    ("G3c", 1),
+    ("G1b", 0),
+    ("G2b", 1),
+    ("G2c", 1),
+    ("G1c", 0),
+    ("G1b", 1),
+    ("G1c", 1),
+)
 HEIGHT = [8 * len(part) for part in PARTS]
 
 
@@ -93,6 +140,7 @@
     gram_all,
     matrix,
     inverse,
+    inverse_terms,
     squares_in,
     load_sem,
     send_sem,
@@ -134,21 +182,20 @@
 
     started = []
 
-    def send(index, src, dst, target, sems=None):
-        first, second = (send_sem, recv_sem) if sems is None else sems
+    def send(first, second, src, dst, target):
         copy = pltpu.make_async_remote_copy(
-            src_ref=src,
-            dst_ref=dst,
-            send_sem=first.at[index],
-            recv_sem=second.at[index],
-            device_id=target,
-            device_id_type=MESH,
+            src_ref=src, dst_ref=dst, send_sem=first, recv_sem=second, device_id=target, device_id_type=MESH
         )
         copy.start()
+        return copy
+
+    def misc(index, src, dst, target):
+        copy = send(misc_send.at[index], misc_recv.at[index], src, dst, target)
         started.append(copy)
         return copy
 
-    misc = functools.partial(send, sems=(misc_send, misc_recv))
+    def wait_all(ref, sem):
+        pltpu.make_async_copy(ref, ref, sem).wait()
 
     def left_partial(j):
         pad = PADDED[j]
@@ -214,46 +261,44 @@
     def place(ref, base, half, chunk, side):
         return ref.at[pl.ds(base + ((chunk % 4) * 2 + side) * half, half)]
 
-    def setting(k, phase):
-        axes = AXES[k % 3]
-        first = coord[axes[0]]
-        axis = axes[phase - 1]
-        return axis, coord[axis], 16 * first
+    def first_coord(k):
+        return coord[AXES[k % 3][0]]
+
+    def reduce_setting(k, phase):
+        axis = AXES[k % 3][phase - 1]
+        base, half, inbox = (0, 8, inbox1[k]) if phase == 1 else (16 * first_coord(k), 2, inbox2[k])
+        at = functools.partial(place, partial[k], base, half)
+
+        def out(n, ref, box, shift):
+            sem = recv_sem.at[k, 3 * (phase - 1) + min(n, 2)]
+            send(send_sem.at[k, 0], sem, ref, inbox.at[box], device(axis, shift))
+
+        return coord[axis], at, half, inbox, out
 
     def reduce_start(k, phase):
-        axis, i, base = setting(k, phase)
-        base, half, inbox = (0, 8, inbox1[k]) if phase == 1 else (base, 2, inbox2[k])
-        at = functools.partial(place, partial[k], base, half)
-        n = 0 if phase == 1 else 6
-        up, down = device(axis, 1), device(axis, 3)
-        return [
-            send((k, n), at(i + 2, 0), inbox.at[0], up),
-            send((k, n + 1), at(i + 2, 1), inbox.at[1], down),
-            send((k, n + 2), at(i + 1, 1), inbox.at[2], up),
-            send((k, n + 3), at(i + 3, 0), inbox.at[3], down),
-        ]
-
-    def reduce_relay(k, phase, copies):
-        axis, i, base = setting(k, phase)
-        base, half, inbox = (0, 8, inbox1[k]) if phase == 1 else (base, 2, inbox2[k])
-        n = 0 if phase == 1 else 6
-        for source, chunk, shift in ((0, i + 1, 1), (1, i + 3, 3)):
-            copies[source].wait_recv()
-            ref = place(partial[k], base, half, chunk, source)
-
-            def add(s, ref=ref, source=source):
-                ref[s] += inbox[source, s]
+        i, at, half, inbox, out = reduce_setting(k, phase)
+        out(0, at(i + 2, 0), 0, 1)
+        out(1, at(i + 2, 1), 1, 3)
+        out(2, at(i + 1, 1), 2, 1)
+        out(2, at(i + 3, 0), 3, 3)
+
+    def reduce_relay(k, phase):
+        i, at, half, inbox, out = reduce_setting(k, phase)
+        for side, chunk, shift in ((0, i + 1, 1), (1, i + 3, 3)):
+            wait_all(inbox.at[side], recv_sem.at[k, 3 * (phase - 1) + side])
+            ref = at(chunk, side)
+
+            def add(s, ref=ref, side=side):
+                ref[s] += inbox[side, s]
 
             each(half, add)
-            copies.append(send((k, n + 4 + source), ref, inbox.at[4 + source], device(axis, shift)))
-
-    def reduce_finish(k, phase, copies):
-        axis, i, base = setting(k, phase)
-        base, half, inbox = (0, 8, inbox1[k]) if phase == 1 else (base, 2, inbox2[k])
-        for n in (2, 3, 4, 5):
-            copies[n].wait_recv()
+            out(2, ref, 4 + side, shift)
+
+    def reduce_finish(k, phase):
+        i, at, half, inbox, out = reduce_setting(k, phase)
+        wait_all(inbox.at[2:6], recv_sem.at[k, 3 * (phase - 1) + 2])
         for side, near, relayed in ((0, 3, 4), (1, 2, 5)):
-            ref = place(partial[k], base, half, i, side)
+            ref = at(i, side)
 
             def add(s, ref=ref, near=near, relayed=relayed):
                 ref[s] += inbox[near, s] + inbox[relayed, s]
@@ -265,55 +310,67 @@
         return 4 * coord[axes[1]] + coord[axes[2]]
 
     def last_reduce_start(k):
-        axis, i, base = setting(k, 3)
-        base = base + 4 * coord[AXES[k % 3][1]]
-        return [
-            send((k, 11 + s), partial[k].at[base + (i + s) % 4], inbox3[k].at[s - 1], device(axis, s))
-            for s in (1, 2, 3)
-        ]
-
-    def last_reduce_finish(k, copies):
-        for copy in copies:
-            copy.wait_recv()
-        mine = partial[k][16 * coord[AXES[k % 3][0]] + own(k)]
+        axes = AXES[k % 3]
+        base, i = 16 * coord[axes[0]] + 4 * coord[axes[1]], coord[axes[2]]
+        for s in (1, 2, 3):
+            ref = partial[k].at[base + (i + s) % 4]
+            send(send_sem.at[k, 0], recv_sem.at[k, 6], ref, inbox3[k].at[s - 1], device(axes[2], s))
+
+    def last_reduce_finish(k):
+        wait_all(inbox3[k], recv_sem.at[k, 6])
+        mine = partial[k][16 * first_coord(k) + own(k)]
         summed[k][own(k)] = (mine + inbox3[k][0]) + (inbox3[k][1] + inbox3[k][2])
 
     def first_gather_start(k):
-        axis, _, _ = setting(k, 3)
         ref = summed[k].at[own(k)]
-        return [send((k, 14 + s), ref, ref, device(axis, s)) for s in (1, 2, 3)]
+        for s in (1, 2, 3):
+            send(send_sem.at[k, 1], recv_sem.at[k, 7], ref, ref, device(AXES[k % 3][2], s))
+
+    def first_gather_finish(k):
+        wait_all(summed[k].at[0:3], recv_sem.at[k, 7])
+
+    def gather_setting(k, phase):
+        axis = AXES[k % 3][phase - 1]
+        ref, half, first = (factor[k], 8, 11) if phase == 1 else (summed[k], 2, 8)
+        at = functools.partial(place, ref, 0, half)
+
+        def out(n, there, shift):
+            send(send_sem.at[k, 1], recv_sem.at[k, first + n], there, there, device(axis, shift))
+
+        def arrived(n):
+            wait_all(ref.at[0:half] if n < 2 else ref.at[0 : 4 * half], recv_sem.at[k, first + n])
+
+        return coord[axis], at, out, arrived
 
     def gather_start(k, phase):
-        axis, i, _ = setting(k, phase)
-        ref, half, n = (factor[k], 8, 24) if phase == 1 else (summed[k], 2, 18)
-        at = functools.partial(place, ref, 0, half)
-        up, down = device(axis, 1), device(axis, 3)
-        return [
-            send((k, n), at(i, 0), at(i, 0), up),
-            send((k, n + 1), at(i, 1), at(i, 1), down),
-            send((k, n + 2), at(i, 1), at(i, 1), up),
-            send((k, n + 3), at(i, 0), at(i, 0), down),
-        ]
-
-    def gather_relay(k, phase, copies):
-        axis, i, _ = setting(k, phase)
-        ref, half, n = (factor[k], 8, 24) if phase == 1 else (summed[k], 2, 18)
-        at = functools.partial(place, ref, 0, half)
-        copies[0].wait_recv()
-        copies.append(send((k, n + 4), at(i + 3, 0), at(i + 3, 0), device(axis, 1)))
-        copies[1].wait_recv()
-        copies.append(send((k, n + 5), at(i + 1, 1), at(i + 1, 1), device(axis, 3)))
-
-    def gather_finish(k, copies):
-        for n in (2, 3, 4, 5):
-            copies[n].wait_recv()
+        i, at, out, arrived = gather_setting(k, phase)
+        out(0, at(i, 0), 1)
+        out(1, at(i, 1), 3)
+        out(2, at(i, 1), 1)
+        out(2, at(i, 0), 3)
+
+    def gather_relay(k, phase):
+        i, at, out, arrived = gather_setting(k, phase)
+        arrived(0)
+        out(2, at(i + 3, 0), 1)
+        arrived(1)
+        out(2, at(i + 1, 1), 3)
+
+    def gather_finish(k, phase):
+        gather_setting(k, phase)[3](2)
 
     def apply_inverse(k):
-        base = 16 * coord[AXES[k % 3][0]]
-        for slot, (j, _) in enumerate(PARTS[k]):
-            rows = slice(slot * 8, slot * 8 + 8)
-            value = summed[k][:, rows, :].reshape(128, RANK)
-            factor[k][pl.ds(base, 16), rows, :] = nt_dot(value, inverse[j], HIGHEST).reshape(16, 8, RANK)
+        base = 16 * first_coord(k)
+        for j in range(3):
+            slots = [slot for slot, (other, _) in enumerate(PARTS[k]) if other == j]
+            if not slots:
+                continue
+            rows = slice(slots[0] * 8, slots[-1] * 8 + 8)
+            count = 8 * len(slots)
+            high, low = split(summed[k][:, rows, :].reshape(16 * count, RANK))
+            product = nt_dot(jnp.concatenate([high, low], axis=0), inverse_terms[j])
+            product = product[: 16 * count, :RANK] + (product[: 16 * count, RANK:] + product[16 * count :, :RANK])
+            factor[k][pl.ds(base, 16), rows, :] = product.reshape(16, count, RANK)
 
     def gram_scatter():
         x = coord[0]
@@ -343,9 +400,6 @@
             copy.wait_recv()
         return misc(15, gram_all.at[core], gram_all.at[core], partner)
 
-    lane = lax.broadcasted_iota(jnp.int32, (8, RANK), 1)
-    sublane = lax.broadcasted_iota(jnp.int32, (8, RANK), 0)
-
     def gram_finish(copy):
         copy.wait_recv()
         row = lax.broadcasted_iota(jnp.int32, (RANK, RANK), 0)
@@ -354,150 +408,132 @@
             matrix[j, :, 0:RANK] = gram_all[:, :, j].reshape(RANK, RANK)
             matrix[j, :, RANK:] = (row == col).astype(F32)
 
-    def eliminate(block):
-        first = pl.multiple_of(block * 8, 8)
-        panels = []
+    def eliminate(piece):
+        first, start = piece // 4 * 32, piece * 8
+        stop = first + 32
+        count = stop - start
+        a = matrix[:, start:stop, 0:RANK]
+        x = matrix[:, start:stop, RANK:]
+        rows = lax.broadcasted_iota(jnp.int32, (3, count, RANK), 1)
+        columns = [jnp.broadcast_to(a[:, :, start + n : start + n + 1], (3, count, RANK)) for n in range(8)]
+        pivots = []
+        for n in range(8):
+            pivot = columns[n][:, n : n + 1, :]
+            pivots.append(pivot)
+            scale = 1.0 / jnp.broadcast_to(pivot, (3, 8, RANK))
+            ratio = jnp.where(rows > n, columns[n] * scale[:, 0:1, :], 0.0)
+            for later in range(n + 1, 8):
+                columns[later] = columns[later] - ratio * columns[later][:, n : n + 1, :]
+            a = a - ratio * a[:, n : n + 1, :]
+            x = x - ratio * x[:, n : n + 1, :]
+        scale = 1.0 / jnp.sqrt(jnp.concatenate(pivots, axis=1))
+        matrix[:, start : start + 8, 0:RANK] = a[:, 0:8] * scale
+        inverse[:, start : start + 8, :] = x[:, 0:8] * scale
+        if count > 8:
+            matrix[:, start + 8 : stop, 0:RANK] = a[:, 8:]
+            matrix[:, start + 8 : stop, RANK:] = x[:, 8:]
+        elif stop < RANK:
+            lane = lax.broadcasted_iota(jnp.int32, (32, RANK), 1)
+            for j in range(3):
+                panel = jnp.where(lane >= stop, matrix[j, first:stop, 0:RANK], 0.0)
+                both = jnp.concatenate([panel, inverse[j, first:stop, :]], axis=1)
+                matrix[j, stop:] = matrix[j, stop:] - tn_dot(panel, both, HIGHEST)[stop:]
+        else:
+            for j in range(3):
+                high, low = split(inverse[j])
+                inverse_terms[j, 0:RANK] = high
+                inverse_terms[j, RANK:] = low
+
+    def basis_all():
         for j in range(3):
-            both = matrix[j, pl.ds(first, 8), :]
-            panels.append([pltpu.roll(both[:, 0:RANK], (RANK - first) % RANK, 1), both[:, RANK:]])
-        for step in range(8):
-            for j in range(3):
-                a, x = panels[j]
-                pivot = jnp.broadcast_to(a[step : step + 1, step : step + 1], (8, RANK))
-                scale = 1.0 / jnp.sqrt(pivot)
-                column = jnp.broadcast_to(a[:, step : step + 1], (8, RANK)) * scale
-                column = jnp.where(sublane > step, column, 0.0)
-                row_a = jnp.broadcast_to(a[step : step + 1, :], (8, RANK)) * scale
-                row_x = jnp.broadcast_to(x[step : step + 1, :], (8, RANK)) * scale
-                here = sublane == step
-                panels[j] = [
-                    jnp.where(here, row_a, a - column * row_a),
-                    jnp.where(here, row_x, x - column * row_x),
-                ]
-        for j in range(3):
-            a, x = panels[j]
-            a = pltpu.roll(a, first, 1)
-            a = jnp.where(lane >= first + 8, a, 0.0)
-            inverse[j, pl.ds(first, 8), :] = x
-            matrix[j] = matrix[j] - tn_dot(a, jnp.concatenate([a, x], axis=1), HIGHEST)
-
-    def eliminate_blocks(start, stop):
-        def step(block, carry):
-            eliminate(block)
-            return carry
-
-        lax.fori_loop(start, stop, step, 0)
-
-    wave0 = (0, 1, 2)
-    wave1 = (3, 4, 5)
-    flying = {}
-
-    pl.semaphore_wait(barrier, len(peers))
-    left_copies = [left_partial(0), left_partial(1)]
-    left_finish(0, left_copies[0])
-    factor_part(0)
-    flying[0] = reduce_start(0, 1)
-    left_finish(1, left_copies[1])
-    for k in (1, 2):
-        factor_part(k)
-        flying[k] = reduce_start(k, 1)
-    left_copies.append(left_partial(2))
-    for j in (0, 1):
-        gram_partial(j)
-    left_finish(2, left_copies[2])
-    gram_partial(2)
-    gram_copies = gram_scatter()
-    for k in wave0:
-        reduce_relay(k, 1, flying[k])
-    for k in wave1:
-        factor_part(k)
-        flying[k] = reduce_start(k, 1)
-    gram_copies = gram_exchange(gram_copies, (gram_in1, coord[0]), gram_in2, (gram.at[core, coord[0]], gram_sum.at[0]), 1, 5)
-    for k in wave0:
-        reduce_finish(k, 1, flying[k])
-        flying[k] = reduce_start(k, 2)
-    gram_copies = gram_exchange(gram_copies, (gram_in2, coord[1]), gram_in3, (gram_sum.at[0], gram_sum.at[1]), 2, 8)
-    for k in wave0:
-        reduce_relay(k, 2, flying[k])
-    for k in wave1:
-        reduce_relay(k, 1, flying[k])
-    gram_copies = gram_gather(gram_copies)
-    for k in wave0:
-        reduce_finish(k, 2, flying[k])
-        flying[k] = last_reduce_start(k)
-    gram_copy = gram_swap(gram_copies)
-    gram_finish(gram_copy)
-    eliminate_blocks(0, 4)
-    for k in wave0:
-        last_reduce_finish(k, flying[k])
-        flying[k] = first_gather_start(k)
-    for k in wave1:
-        reduce_finish(k, 1, flying[k])
-        flying[k] = reduce_start(k, 2)
-    eliminate_blocks(4, 7)
-    for k in wave0:
-        gather_finish_direct(flying[k])
-        flying[k] = gather_start(k, 2)
-    for k in wave1:
-        reduce_relay(k, 2, flying[k])
-    eliminate_blocks(7, 10)
-    for k in wave0:
-        gather_relay(k, 2, flying[k])
-    for k in wave1:
-        reduce_finish(k, 2, flying[k])
-        flying[k] = last_reduce_start(k)
-    eliminate_blocks(10, 16)
-    for k in wave0:
-        gather_finish(k, flying[k])
-        apply_inverse(k)
-        flying[k] = gather_start(k, 1)
-    for k in wave1:
-        last_reduce_finish(k, flying[k])
-        flying[k] = first_gather_start(k)
-    for j in range(3):
-        basis[j][...] = nt_dot(left_in[j][...], inverse[j], HIGHEST)[0 : ROWS[j]]
-    for k in wave1:
-        gather_finish_direct(flying[k])
-        flying[k] = gather_start(k, 2)
-    for k in wave0:
-        gather_relay(k, 1, flying[k])
-    for k in wave1:
-        gather_relay(k, 2, flying[k])
-    for k in wave1:
-        gather_finish(k, flying[k])
-        apply_inverse(k)
-        flying[k] = gather_start(k, 1)
-    for k in wave0:
-        gather_finish(k, flying[k])
+            basis[j][...] = nt_dot(left_in[j][...], inverse[j], HIGHEST)[0 : ROWS[j]]
+
     sums = [jnp.zeros((8, RANK), F32) for _ in range(3)]
 
-    def add_squares(k, sums):
+    def add_squares(k):
         for slot, (j, _) in enumerate(PARTS[k]):
+
             def step(i, total, slot=slot):
                 value = factor[k][pl.ds(i * 8, 8), slot * 8 : slot * 8 + 8, :]
                 return total + jnp.sum(value * value, axis=0)
 
             sums[j] = lax.fori_loop(0, 8, step, sums[j])
 
-    for k in wave0:
-        add_squares(k, sums)
-    for k in wave1:
-        gather_relay(k, 1, flying[k])
-    for k in wave1:
-        gather_finish(k, flying[k])
-        add_squares(k, sums)
+    held = {}
+
+    def run(name, value):
+        parts = range(3 * value, 3 * value + 3)
+        if name == "left":
+            held["left", value] = left_partial(value)
+        elif name == "finish":
+            left_finish(value, held["left", value])
+        elif name == "gram":
+            if value == 0:
+                for j in range(3):
+                    gram_partial(j)
+                held["gram"] = gram_scatter()
+            elif value == 1:
+                sent = (gram.at[core, coord[0]], gram_sum.at[0])
+                held["gram"] = gram_exchange(held["gram"], (gram_in1, coord[0]), gram_in2, sent, 1, 5)
+            elif value == 2:
+                sent = (gram_sum.at[0], gram_sum.at[1])
+                held["gram"] = gram_exchange(held["gram"], (gram_in2, coord[1]), gram_in3, sent, 2, 8)
+            elif value == 3:
+                held["gram"] = gram_gather(held["gram"])
+            elif value == 4:
+                held["gram"] = gram_swap(held["gram"])
+            else:
+                gram_finish(held["gram"])
+        elif name == "chol":
+            for piece in range(2 * value, 2 * value + 2):
+                eliminate(piece)
+            if value == 7:
+                basis_all()
+        for k in parts:
+            if name == "R1a":
+                factor_part(k)
+                reduce_start(k, 1)
+            elif name == "R1b":
+                reduce_relay(k, 1)
+            elif name == "R1c":
+                reduce_finish(k, 1)
+                reduce_start(k, 2)
+            elif name == "R2b":
+                reduce_relay(k, 2)
+            elif name == "R2c":
+                reduce_finish(k, 2)
+                last_reduce_start(k)
+            elif name == "R3c":
+                last_reduce_finish(k)
+                first_gather_start(k)
+            elif name == "G3c":
+                first_gather_finish(k)
+                gather_start(k, 2)
+            elif name == "G2b":
+                gather_relay(k, 2)
+            elif name == "G2c":
+                gather_finish(k, 2)
+                apply_inverse(k)
+                gather_start(k, 1)
+            elif name == "G1b":
+                gather_relay(k, 1)
+            elif name == "G1c":
+                gather_finish(k, 1)
+                add_squares(k)
+
+    pl.semaphore_wait(barrier, len(peers))
+    for name, value in PLAN:
+        run(name, value)
     rows = [jnp.sum(value, axis=0, keepdims=True) for value in sums]
     squares_in[0] = jnp.concatenate(rows + [jnp.zeros((5, RANK), F32)], axis=0)
     copy = misc(16, squares_in.at[0], squares_in.at[1], partner)
+    for k in range(N_PARTS):
+        for side in range(2):
+            wait_all(partial[k].at[0:63], send_sem.at[k, side])
     copy.wait_recv()
     squares[...] = squares_in[0] + squares_in[1]
     for copy in started:
         copy.wait_send()
-
-
-def gather_finish_direct(copies):
-    for copy in copies:
-        copy.wait_recv()
 
 
 def update_kernel(
@@ -537,14 +573,13 @@
         moment = (value * (1.0 - DECAY)).astype(BF16)
         rows_in[j][2 * pad :, 0:RANK] = moment
         rows_in[j][2 * pad :, RANK:] = jnp.zeros((pad, RANK), BF16)
-    waited = [False] * 3
-    stores = []
-    for k in range(N_PARTS):
-        for slot, (j, unit) in enumerate(PARTS[k]):
-            if not waited[j]:
-                loads[j].wait()
-                waited[j] = True
-            rows, pad = ROWS[j], PADDED[j]
+    where = {unit: (k, slot) for k, part in enumerate(PARTS) for slot, unit in enumerate(part)}
+    for group, (j, units) in enumerate(GROUPS):
+        if units[0] == 0:
+            loads[j].wait()
+        rows, pad = ROWS[j], PADDED[j]
+        for unit in units:
+            k, slot = where[j, unit]
             start = unit * UNIT
             width = min(UNIT, COLS[j] - start)
             value = factor[k][0 : width // 8, slot * 8 : slot * 8 + 8, :].reshape(width, RANK)
@@ -556,18 +591,15 @@
             change_box[j][:, cols] = change
             moment_box[j][:, cols] = buffer[j][:, cols] - product[2 * pad : 2 * pad + rows]
             weight_box[j][:, cols] = (weight_in[j][:, cols].astype(F32) - change).astype(BF16)
-            pairs = (
-                (right_box[j].at[cols, :], right_out[j].at[cols, :]),
-                (change_box[j].at[:, cols], change_out[j].at[:, cols]),
-                (moment_box[j].at[:, cols], moment_out[j].at[:, cols]),
-                (weight_box[j].at[:, cols], weight_out[j].at[:, cols]),
-            )
-            for n, (src, dst) in enumerate(pairs):
-                copy = pltpu.make_async_copy(src, dst, store_sem.at[k, slot, n])
-                copy.start()
-                stores.append(copy)
-    for copy in stores:
-        copy.wait()
+        cols = slice(units[0] * UNIT, min(units[-1] * UNIT + UNIT, COLS[j]))
+        pltpu.make_async_copy(right_box[j].at[cols, :], right_out[j].at[cols, :], store_sem.at[j, 0]).start()
+        for n, (box, out) in enumerate(((change_box, change_out), (moment_box, moment_out), (weight_box, weight_out))):
+            pltpu.make_async_copy(box[j].at[:, cols], out[j].at[:, cols], store_sem.at[j, n + 1]).start()
+    for j in range(3):
+        for n, (box, out) in enumerate(
+            ((right_box, right_out), (change_box, change_out), (moment_box, moment_out), (weight_box, weight_out))
+        ):
+            pltpu.make_async_copy(box[j], out[j], store_sem.at[j, n]).wait()
 
 
 def local(
@@ -626,10 +658,11 @@
             vmem((2, 4, 3, 16, RANK), F32),
             vmem((3, RANK, 2 * RANK), F32),
             vmem((3, RANK, RANK), F32),
+            vmem((3, 2 * RANK, RANK), BF16),
             vmem((2, 8, RANK), F32),
             dma((3, 3, 3)),
-            dma((N_PARTS, 30)),
-            dma((N_PARTS, 30)),
+            dma((N_PARTS, 2)),
+            dma((N_PARTS, 14)),
             dma((17,)),
             dma((17,)),
         ],
@@ -656,7 +689,7 @@
             [vmem((ROWS[j], COLS[j]), F32) for j in range(3)],
             [vmem((3 * PADDED[j], 2 * RANK), BF16) for j in range(3)],
             dma((3,)),
-            dma((N_PARTS, max(PER_PART), 4)),
+            dma((3, 4)),
         ],
         compiler_params=pltpu.CompilerParams(vmem_limit_bytes=44 * 2**20),
         name="update",

time: 115 us -> 90.9 us (0.79)
  Pallas kernels: 112 us -> 88.7 us
    pallas_call x1, Pallas kernels: 103 us -> 80.5 us  [local(): pl.pallas_call(reduce_kernel, out_shape=placed, in_specs=[[anywhere] * 3]...]
where the time goes in v2:
time: 90.9 us; the launch traced here: 89.5 us
  Pallas kernels  88.7 us (98%)
    pallas_call x1, Pallas kernels, local(): pl.pallas_call(reduce_kernel, out_shape=placed, in_specs=[[anywhere] * 3]...  80.5 us
    pallas_call x1, Pallas kernels, local(): pl.pallas_call(update_kernel, out_shape=results, in_specs=[[anywhere] * 3...  8.2 us

profile of v2, /device:TPU:0, one launch (start us, length us, event | category | flops | bytes accessed | tf_op | source)
XLA Modules:
  0.0 89.5 jit_solution(6251525116647536777)
XLA Ops:
  0.6 80.5 %reduce.1 = (f32[64,24,128]{2,1,0:T(8,128)S(1)}, f32[64,24,128]{2,1,0:T(8,128)S(1)}, f32[64,24,128]{2,1,0:T(8,128)S(1)}, f32[64,40,128]{2,1,0:T(8,128)S(1)}, f32...) custom-call(f32[216,2560]{1,0:T(8,128)} %momentum_0_.1, ...), custom_call_target="tpu_custom_call" | custom-call | tf_op jit(solution)/shard_map/reduce/pallas_call | solution.py:635
  81.1 8.2 %update.1 = (f32[216,2560]{1,0:T(8,128)}, f32[80,2560]{1,0:T(8,128)}, f32[80,6912]{1,0:T(8,128)}, bf16[216,2560]{1,0:T(8,128)(2,1)}, bf16[80,2560]{1,0:T(8,128)(...) custom-call(bf16[216,2560]{1,0:T(8,128)(2,1)} %weight_0_.1, ...), custom_call_target="tpu_custom_call" | custom-call | tf_op jit(solution)/shard_map/update/pallas_call | solution.py:679

commit v3 on v2

--- a/solution.py
+++ b/solution.py
@@ -26,7 +26,7 @@
 AXES = ((0, 1, 2), (1, 2, 0), (2, 0, 1))
 TERMS = tuple(3 * rows + (-3 * rows) % 128 for rows in PADDED)
 
-PER_PART = (3, 5)
+PER_PART = (3, 3, 2)
 
 
 def make_parts():
@@ -47,46 +47,54 @@
 PLAN = (
     ("left", 0),
     ("left", 1),
-    ("finish", 0),
-    ("finish", 1),
     ("R1a", 0),
     ("left", 2),
-    ("finish", 2),
+    ("R1a", 1),
     ("gram", 0),
     ("R1b", 0),
+    ("R1a", 2),
     ("gram", 1),
-    ("R1a", 1),
+    ("R1b", 1),
+    ("R1c", 0),
+    ("R1b", 2),
     ("gram", 2),
-    ("R1c", 0),
+    ("R1c", 1),
+    ("R2b", 0),
     ("gram", 3),
-    ("R2b", 0),
+    ("R1c", 2),
+    ("R2b", 1),
+    ("R2c", 0),
+    ("R2b", 2),
     ("gram", 4),
-    ("R1b", 1),
+    ("R2c", 1),
     ("gram", 5),
     ("chol", 0),
-    ("R2c", 0),
+    ("R3c", 0),
+    ("R2c", 2),
     ("chol", 1),
-    ("R1c", 1),
-    ("R3c", 0),
     ("chol", 2),
-    ("R2b", 1),
+    ("R3c", 1),
     ("chol", 3),
     ("G3c", 0),
     ("chol", 4),
-    ("R2c", 1),
+    ("R3c", 2),
+    ("chol", 5),
+    ("G3c", 1),
     ("G2b", 0),
-    ("chol", 5),
-    ("R3c", 1),
     ("chol", 6),
     ("chol", 7),
+    ("G3c", 2),
+    ("G2b", 1),
     ("G2c", 0),
-    ("G3c", 1),
+    ("G2b", 2),
+    ("G2c", 1),
     ("G1b", 0),
-    ("G2b", 1),
-    ("G2c", 1),
+    ("G2c", 2),
+    ("G1b", 1),
+    ("G1b", 2),
     ("G1c", 0),
-    ("G1b", 1),
     ("G1c", 1),
+    ("G1c", 2),
 )
 HEIGHT = [8 * len(part) for part in PARTS]
 
@@ -116,19 +124,21 @@
     momentum,
     gradient,
     right,
+    weight,
     factor,
     buffer,
     basis,
     squares,
+    weight_in,
     partial,
     summed,
     inbox1,
     inbox2,
     inbox3,
+    pairs,
     grad_in,
     right_in,
     terms,
-    right_terms,
     left,
     left_in,
     left_terms,
@@ -175,6 +185,10 @@
             start += span
         loads.append(steps)
 
+    weight_loads = [pltpu.make_async_copy(weight[j], weight_in[j], load_sem.at[j, 3, 0]) for j in range(3)]
+    for copy in weight_loads:
+        copy.start()
+
     barrier = pltpu.get_barrier_semaphore()
     peers = [device(axis, shift) for axis in range(3) for shift in (1, 2, 3)] + [partner]
     for peer in peers:
@@ -196,6 +210,8 @@
 
     def wait_all(ref, sem):
         pltpu.make_async_copy(ref, ref, sem).wait()
+
+    held = {}
 
     def left_partial(j):
         pad = PADDED[j]
@@ -214,16 +230,10 @@
                 terms[j][0:pad, cols] = high
                 terms[j][pad : 2 * pad, cols] = low
                 terms[j][2 * pad : 3 * pad, cols] = high
-                high, low = split(right_in[j][cols, :])
-                right_terms[j][cols, 0:RANK] = high
-                right_terms[j][cols, RANK : 2 * RANK] = low
 
             each(span // 256, prepare)
-            product = jnp.dot(
-                terms[j][0 : 2 * pad, start : start + span],
-                right_terms[j][start : start + span, :],
-                preferred_element_type=F32,
-            )
+            right_terms = jnp.concatenate(split(right_in[j][start : start + span, :]), axis=1)
+            product = jnp.dot(terms[j][0 : 2 * pad, start : start + span], right_terms, preferred_element_type=F32)
             product = product[0:pad, 0:RANK] + (product[0:pad, RANK:] + product[pad:, 0:RANK])
             total = product if total is None else total + product
         left[j][...] = total
@@ -254,7 +264,16 @@
         product = jnp.dot(left_terms[j][:, 0 : 3 * PADDED[j]], terms[j][:, cols], preferred_element_type=F32)
         partial[k][:, slot * 8 : slot * 8 + 8, :] = product.T.reshape(64, 8, RANK)
 
+    finished = set()
+
+    def finish(j):
+        if j not in finished:
+            finished.add(j)
+            left_finish(j, held["left", j])
+
     def factor_part(k):
+        for j in sorted({j for j, _ in PARTS[k]}):
+            finish(j)
         for slot in range(len(PARTS[k])):
             factor_unit(k, slot)
 
@@ -287,47 +306,35 @@
         for side, chunk, shift in ((0, i + 1, 1), (1, i + 3, 3)):
             wait_all(inbox.at[side], recv_sem.at[k, 3 * (phase - 1) + side])
             ref = at(chunk, side)
-
-            def add(s, ref=ref, side=side):
-                ref[s] += inbox[side, s]
-
-            each(half, add)
+            ref[...] += inbox[side]
             out(2, ref, 4 + side, shift)
 
     def reduce_finish(k, phase):
         i, at, half, inbox, out = reduce_setting(k, phase)
         wait_all(inbox.at[2:6], recv_sem.at[k, 3 * (phase - 1) + 2])
         for side, near, relayed in ((0, 3, 4), (1, 2, 5)):
-            ref = at(i, side)
-
-            def add(s, ref=ref, near=near, relayed=relayed):
-                ref[s] += inbox[near, s] + inbox[relayed, s]
-
-            each(half, add)
-
-    def own(k):
+            at(i, side)[...] += inbox[near] + inbox[relayed]
+
+    def exchange_setting(k):
         axes = AXES[k % 3]
-        return 4 * coord[axes[1]] + coord[axes[2]]
-
-    def last_reduce_start(k):
-        axes = AXES[k % 3]
-        base, i = 16 * coord[axes[0]] + 4 * coord[axes[1]], coord[axes[2]]
-        for s in (1, 2, 3):
-            ref = partial[k].at[base + (i + s) % 4]
-            send(send_sem.at[k, 0], recv_sem.at[k, 6], ref, inbox3[k].at[s - 1], device(axes[2], s))
-
-    def last_reduce_finish(k):
-        wait_all(inbox3[k], recv_sem.at[k, 6])
-        mine = partial[k][16 * first_coord(k) + own(k)]
-        summed[k][own(k)] = (mine + inbox3[k][0]) + (inbox3[k][1] + inbox3[k][2])
-
-    def first_gather_start(k):
-        ref = summed[k].at[own(k)]
-        for s in (1, 2, 3):
-            send(send_sem.at[k, 1], recv_sem.at[k, 7], ref, ref, device(AXES[k % 3][2], s))
-
-    def first_gather_finish(k):
-        wait_all(summed[k].at[0:3], recv_sem.at[k, 7])
+        second, third = coord[axes[1]], coord[axes[2]]
+        shifts = (1 + 2 * (third % 2), 3 - 2 * (third % 2))
+        return axes[2], shifts, pl.ds(16 * coord[axes[0]] + 4 * second, 4), pl.ds(4 * second, 4)
+
+    def exchange_start(k):
+        axis, shifts, mine, _ = exchange_setting(k)
+        send(send_sem.at[k, 2], recv_sem.at[k, 6], partial[k].at[mine], inbox3[k].at[0], device(axis, shifts[0]))
+
+    def exchange_middle(k):
+        axis, shifts, mine, _ = exchange_setting(k)
+        wait_all(inbox3[k].at[0], recv_sem.at[k, 6])
+        pairs[k][...] = partial[k][mine] + inbox3[k][0]
+        send(send_sem.at[k, 3], recv_sem.at[k, 7], pairs[k], inbox3[k].at[1], device(axis, shifts[1]))
+
+    def exchange_finish(k):
+        _, _, _, there = exchange_setting(k)
+        wait_all(inbox3[k].at[1], recv_sem.at[k, 7])
+        summed[k][there] = pairs[k][...] + inbox3[k][1]
 
     def gather_setting(k, phase):
         axis = AXES[k % 3][phase - 1]
@@ -452,24 +459,20 @@
 
     def add_squares(k):
         for slot, (j, _) in enumerate(PARTS[k]):
-
-            def step(i, total, slot=slot):
-                value = factor[k][pl.ds(i * 8, 8), slot * 8 : slot * 8 + 8, :]
-                return total + jnp.sum(value * value, axis=0)
-
-            sums[j] = lax.fori_loop(0, 8, step, sums[j])
-
-    held = {}
+            total = None
+            for start in range(0, 64, 8):
+                value = factor[k][start : start + 8, slot * 8 : slot * 8 + 8, :]
+                total = value * value if total is None else total + value * value
+            sums[j] = sums[j] + jnp.sum(total, axis=0)
 
     def run(name, value):
         parts = range(3 * value, 3 * value + 3)
         if name == "left":
             held["left", value] = left_partial(value)
-        elif name == "finish":
-            left_finish(value, held["left", value])
         elif name == "gram":
             if value == 0:
                 for j in range(3):
+                    finish(j)
                     gram_partial(j)
                 held["gram"] = gram_scatter()
             elif value == 1:
@@ -502,12 +505,11 @@
                 reduce_relay(k, 2)
             elif name == "R2c":
                 reduce_finish(k, 2)
-                last_reduce_start(k)
+                exchange_start(k)
             elif name == "R3c":
-                last_reduce_finish(k)
-                first_gather_start(k)
+                exchange_middle(k)
             elif name == "G3c":
-                first_gather_finish(k)
+                exchange_finish(k)
                 gather_start(k, 2)
             elif name == "G2b":
                 gather_relay(k, 2)
@@ -527,9 +529,13 @@
     rows = [jnp.sum(value, axis=0, keepdims=True) for value in sums]
     squares_in[0] = jnp.concatenate(rows + [jnp.zeros((5, RANK), F32)], axis=0)
     copy = misc(16, squares_in.at[0], squares_in.at[1], partner)
+    for load in weight_loads:
+        load.wait()
     for k in range(N_PARTS):
-        for side in range(2):
-            wait_all(partial[k].at[0:63], send_sem.at[k, side])
+        wait_all(partial[k].at[0:60], send_sem.at[k, 0])
+        wait_all(pairs[k], send_sem.at[k, 2])
+        wait_all(pairs[k], send_sem.at[k, 3])
+        wait_all(partial[k].at[0:60], send_sem.at[k, 1])
     copy.wait_recv()
     squares[...] = squares_in[0] + squares_in[1]
     for copy in started:
@@ -537,7 +543,7 @@
 
 
 def update_kernel(
-    weight,
+    weight_in,
     factor,
     buffer,
     basis,
@@ -546,18 +552,13 @@
     weight_out,
     right_out,
     change_out,
-    weight_in,
     moment_box,
     weight_box,
     right_box,
     change_box,
     rows_in,
-    load_sem,
     store_sem,
 ):
-    loads = [pltpu.make_async_copy(weight[j], weight_in[j], load_sem.at[j]) for j in range(3)]
-    for copy in loads:
-        copy.start()
     scale = 1.0 / (jnp.sqrt(squares[...]) + EPSILON)
     for j in range(3):
         rows, pad = ROWS[j], PADDED[j]
@@ -574,9 +575,7 @@
         rows_in[j][2 * pad :, 0:RANK] = moment
         rows_in[j][2 * pad :, RANK:] = jnp.zeros((pad, RANK), BF16)
     where = {unit: (k, slot) for k, part in enumerate(PARTS) for slot, unit in enumerate(part)}
-    for group, (j, units) in enumerate(GROUPS):
-        if units[0] == 0:
-            loads[j].wait()
+    for j, units in GROUPS:
         rows, pad = ROWS[j], PADDED[j]
         for unit in units:
             k, slot = where[j, unit]
@@ -629,24 +628,25 @@
     factor_shapes = [jax.ShapeDtypeStruct((64, HEIGHT[k], RANK), F32) for k in range(N_PARTS)]
     buffer_shapes = [jax.ShapeDtypeStruct((ROWS[j], COLS[j]), F32) for j in range(3)]
     basis_shapes = [jax.ShapeDtypeStruct((ROWS[j], RANK), F32) for j in range(3)]
-    middle = [factor_shapes, buffer_shapes, basis_shapes, jax.ShapeDtypeStruct((8, RANK), F32)]
+    weight_shapes = [jax.ShapeDtypeStruct((ROWS[j], COLS[j]), BF16) for j in range(3)]
+    middle = [factor_shapes, buffer_shapes, basis_shapes, jax.ShapeDtypeStruct((8, RANK), F32), weight_shapes]
     placed = jax.tree.map(lambda s: vmem(s.shape, s.dtype), middle)
     terms_cols = [UNIT * count for count in UNITS]
-    factor, buffer, basis, squares = pl.pallas_call(
+    middle = pl.pallas_call(
         reduce_kernel,
         out_shape=placed,
-        in_specs=[[anywhere] * 3] * 3,
+        in_specs=[[anywhere] * 3] * 4,
         out_specs=jax.tree.map(lambda s: inside, middle),
         scratch_shapes=[
             each_part((64,)),
             each_part((16,)),
             each_part((6, 8)),
             each_part((6, 2)),
-            each_part((3,)),
+            each_part((2, 4)),
+            each_part((4,)),
             [vmem((ROWS[j], COLS[j]), BF16) for j in range(3)],
             [vmem((COLS[j], RANK), F32) for j in range(3)],
             [vmem((3 * PADDED[j], terms_cols[j]), BF16) for j in range(3)],
-            [vmem((COLS[j], 2 * RANK), BF16) for j in range(3)],
             [vmem((PADDED[j], RANK), F32) for j in range(3)],
             [vmem((PADDED[j], RANK), F32) for j in range(3)],
             [vmem((RANK, TERMS[j]), BF16) for j in range(3)],
@@ -660,38 +660,36 @@
             vmem((3, RANK, RANK), F32),
             vmem((3, 2 * RANK, RANK), BF16),
             vmem((2, 8, RANK), F32),
-            dma((3, 3, 3)),
-            dma((N_PARTS, 2)),
+            dma((3, 4, 3)),
+            dma((N_PARTS, 4)),
             dma((N_PARTS, 14)),
             dma((17,)),
             dma((17,)),
         ],
         compiler_params=pltpu.CompilerParams(
-            collective_id=0, has_side_effects=True, vmem_limit_bytes=50 * 2**20
+            collective_id=0, has_side_effects=True, vmem_limit_bytes=45 * 2**20
         ),
         name="reduce",
-    )(momentum, gradient, right)
+    )(momentum, gradient, right, weight)
     keep = lambda x: pltpu.with_memory_space_constraint(x, vmem)
-    factor, buffer, basis, squares = jax.tree.map(keep, (factor, buffer, basis, squares))
+    factor, buffer, basis, squares, weight = jax.tree.map(keep, tuple(middle))
     matrices = lambda dtype: [jax.ShapeDtypeStruct((ROWS[j], COLS[j]), dtype) for j in range(3)]
     factors = [jax.ShapeDtypeStruct((COLS[j], RANK), F32) for j in range(3)]
     results = [matrices(F32), matrices(BF16), factors, matrices(F32)]
     moment, weight, right, change = pl.pallas_call(
         update_kernel,
         out_shape=results,
-        in_specs=[[anywhere] * 3, [inside] * N_PARTS, [inside] * 3, [inside] * 3, inside],
+        in_specs=[[inside] * 3, [inside] * N_PARTS, [inside] * 3, [inside] * 3, inside],
         out_specs=jax.tree.map(lambda s: anywhere, results),
         scratch_shapes=[
-            [vmem((ROWS[j], COLS[j]), BF16) for j in range(3)],
             [vmem((ROWS[j], COLS[j]), F32) for j in range(3)],
             [vmem((ROWS[j], COLS[j]), BF16) for j in range(3)],
             [vmem((COLS[j], RANK), F32) for j in range(3)],
             [vmem((ROWS[j], COLS[j]), F32) for j in range(3)],
             [vmem((3 * PADDED[j], 2 * RANK), BF16) for j in range(3)],
-            dma((3,)),
             dma((3, 4)),
         ],
-        compiler_params=pltpu.CompilerParams(vmem_limit_bytes=44 * 2**20),
+        compiler_params=pltpu.CompilerParams(vmem_limit_bytes=40 * 2**20),
         name="update",
     )(weight, factor, buffer, basis, squares)
     pick = lambda group: (group[1], group[2], group[0])

time: 90.9 us -> 84 us (0.924)
  Pallas kernels: 88.7 us -> 81.8 us
    pallas_call x1, Pallas kernels: 80.5 us -> 74.9 us  [local(): pl.pallas_call(reduce_kernel, out_shape=placed, in_specs=[[anywhere] * 3]...]
    pallas_call x1, Pallas kernels: 8.2 us -> 6.91 us  [local(): pl.pallas_call(update_kernel, out_shape=results, in_specs=[[inside] * 3,...]
where the time goes in v3:
time: 84 us; the launch traced here: 82.6 us
  Pallas kernels  81.8 us (97%)
  between operations  0.84 us (1%)
    pallas_call x1, Pallas kernels, local(): pl.pallas_call(reduce_kernel, out_shape=placed, in_specs=[[anywhere] * 3]...  74.9 us
    pallas_call x1, Pallas kernels, local(): pl.pallas_call(update_kernel, out_shape=results, in_specs=[[inside] * 3,...  6.91 us

profile of v3, /device:TPU:0, one launch (start us, length us, event | category | flops | bytes accessed | tf_op | source)
XLA Modules:
  0.0 82.6 jit_solution(4867788610464276393)
XLA Ops:
  0.6 74.9 %reduce.1 = (f32[64,24,128]{2,1,0:T(8,128)S(1)}, f32[64,24,128]{2,1,0:T(8,128)S(1)}, f32[64,24,128]{2,1,0:T(8,128)S(1)}, f32[64,24,128]{2,1,0:T(8,128)S(1)}, f32...) custom-call(f32[216,2560]{1,0:T(8,128)} %momentum_0_.1, ...), custom_call_target="tpu_custom_call" | custom-call | tf_op jit(solution)/shard_map/reduce/pallas_call | solution.py:635
  75.5 6.9 %update.1 = (f32[216,2560]{1,0:T(8,128)}, f32[80,2560]{1,0:T(8,128)}, f32[80,6912]{1,0:T(8,128)}, bf16[216,2560]{1,0:T(8,128)(2,1)}, bf16[80,2560]{1,0:T(8,128)(...) custom-call(bf16[216,2560]{1,0:T(8,128)(2,1)S(1)} %get-tuple-element, ...), custom_call_target="tpu_custom_call" | custom-call | tf_op jit(solution)/shard_map/update/pallas_call | solution.py:679

commit v4 on v3

--- a/solution.py
+++ b/solution.py
@@ -26,16 +26,15 @@
 AXES = ((0, 1, 2), (1, 2, 0), (2, 0, 1))
 TERMS = tuple(3 * rows + (-3 * rows) % 128 for rows in PADDED)
 
-PER_PART = (3, 3, 2)
+PER_PART = ((3, 3, 3), (3, 3, 3), (2, 2, 2))
 
 
 def make_parts():
     units = [(matrix, unit) for matrix in range(3) for unit in range(UNITS[matrix])]
     parts = []
-    for count in PER_PART:
-        for _ in range(3):
-            parts.append(units[:count])
-            units = units[count:]
+    for count in sum(PER_PART, ()):
+        parts.append(units[:count])
+        units = units[count:]
     return parts
 
 
@@ -49,51 +48,54 @@
     ("left", 1),
     ("R1a", 0),
     ("left", 2),
+    ("R1b", 0),
+    ("gram", 0),
     ("R1a", 1),
-    ("gram", 0),
-    ("R1b", 0),
+    ("gram", 1),
+    ("R1c", 0),
+    ("R1b", 1),
     ("R1a", 2),
-    ("gram", 1),
-    ("R1b", 1),
-    ("R1c", 0),
+    ("gram", 2),
+    ("R2b", 0),
+    ("R1c", 1),
     ("R1b", 2),
-    ("gram", 2),
-    ("R1c", 1),
-    ("R2b", 0),
     ("gram", 3),
+    ("R2c", 0),
+    ("R2b", 1),
     ("R1c", 2),
-    ("R2b", 1),
-    ("R2c", 0),
-    ("R2b", 2),
+    ("R3c", 0),
     ("gram", 4),
     ("R2c", 1),
     ("gram", 5),
     ("chol", 0),
-    ("R3c", 0),
-    ("R2c", 2),
+    ("R2b", 2),
     ("chol", 1),
+    ("G3c", 0),
     ("chol", 2),
     ("R3c", 1),
     ("chol", 3),
-    ("G3c", 0),
+    ("R2c", 2),
     ("chol", 4),
+    ("G2b", 0),
+    ("chol", 5),
+    ("chol", 6),
+    ("G3c", 1),
+    ("chol", 7),
     ("R3c", 2),
-    ("chol", 5),
-    ("G3c", 1),
-    ("G2b", 0),
-    ("chol", 6),
-    ("chol", 7),
+    ("G2c", 0),
+    ("G2b", 1),
     ("G3c", 2),
-    ("G2b", 1),
-    ("G2c", 0),
+    ("G1b", 0),
     ("G2b", 2),
     ("G2c", 1),
-    ("G1b", 0),
     ("G2c", 2),
     ("G1b", 1),
+    ("G1c", 0),
     ("G1b", 2),
-    ("G1c", 0),
+    ("norms", 0),
+    ("sent", 0),
     ("G1c", 1),
+    ("norms", 1),
     ("G1c", 2),
 )
 HEIGHT = [8 * len(part) for part in PARTS]
@@ -127,7 +129,7 @@
     weight,
     factor,
     buffer,
-    basis,
+    rows_out,
     squares,
     weight_in,
     partial,
@@ -151,12 +153,16 @@
     matrix,
     inverse,
     inverse_terms,
+    basis,
+    norms,
     squares_in,
     load_sem,
     send_sem,
     recv_sem,
     misc_send,
     misc_recv,
+    norm_send,
+    norm_recv,
 ):
     rows_at = lax.axis_index("fsdp")
     core = lax.axis_index("tp")
@@ -366,6 +372,44 @@
     def gather_finish(k, phase):
         gather_setting(k, phase)[3](2)
 
+    sums = [[jnp.zeros((8, RANK), F32) for _ in range(3)] for _ in range(3)]
+    counted = [0] * 3
+
+    def send_norms(part):
+        axis = AXES[part][0]
+        rows = [jnp.sum(value, axis=0, keepdims=True) for value in sums[part]]
+        ref = norms.at[4 * part + coord[axis]]
+        ref[...] = jnp.concatenate(rows + [jnp.zeros((5, RANK), F32)], axis=0)
+        for shift in (1, 2, 3):
+            send(norm_send.at[0], norm_recv.at[part], ref, ref, device(axis, shift))
+
+    def swap_norms():
+        total = None
+        for part in range(3):
+            wait_all(norms.at[0:3], norm_recv.at[part])
+            n = 4 * part
+            value = (norms[n] + norms[n + 1]) + (norms[n + 2] + norms[n + 3])
+            total = value if total is None else total + value
+        squares_in[0] = total
+        held["norms"] = misc(16, squares_in.at[0], squares_in.at[1], partner)
+
+    def finish_norms():
+        held["norms"].wait_recv()
+        total = squares_in[0] + squares_in[1]
+        squares[...] = total
+        scale = 1.0 / (jnp.sqrt(total) + EPSILON)
+        for j in range(3):
+            pad = PADDED[j]
+            value = basis[j][...]
+            step_size = LEARN_RATE * math.sqrt(SHAPE[j][0] / SHAPE[j][1])
+            high, low = split(value * (scale[j : j + 1] * step_size))
+            rows_out[j][0:pad, 0:RANK] = high
+            rows_out[j][0:pad, RANK:] = high
+            rows_out[j][pad : 2 * pad, 0:RANK] = low
+            rows_out[j][pad : 2 * pad, RANK:] = jnp.zeros((pad, RANK), BF16)
+            rows_out[j][2 * pad :, 0:RANK] = (value * (1.0 - DECAY)).astype(BF16)
+            rows_out[j][2 * pad :, RANK:] = jnp.zeros((pad, RANK), BF16)
+
     def apply_inverse(k):
         base = 16 * first_coord(k)
         for j in range(3):
@@ -378,6 +422,11 @@
             product = nt_dot(jnp.concatenate([high, low], axis=0), inverse_terms[j])
             product = product[: 16 * count, :RANK] + (product[: 16 * count, RANK:] + product[16 * count :, :RANK])
             factor[k][pl.ds(base, 16), rows, :] = product.reshape(16, count, RANK)
+            total = jnp.sum((product * product).reshape(2 * count, 8, RANK), axis=0)
+            sums[k % 3][j] = sums[k % 3][j] + total
+        counted[k % 3] += 1
+        if counted[k % 3] == N_PARTS // 3:
+            send_norms(k % 3)
 
     def gram_scatter():
         x = coord[0]
@@ -453,17 +502,7 @@
 
     def basis_all():
         for j in range(3):
-            basis[j][...] = nt_dot(left_in[j][...], inverse[j], HIGHEST)[0 : ROWS[j]]
-
-    sums = [jnp.zeros((8, RANK), F32) for _ in range(3)]
-
-    def add_squares(k):
-        for slot, (j, _) in enumerate(PARTS[k]):
-            total = None
-            for start in range(0, 64, 8):
-                value = factor[k][start : start + 8, slot * 8 : slot * 8 + 8, :]
-                total = value * value if total is None else total + value * value
-            sums[j] = sums[j] + jnp.sum(total, axis=0)
+            basis[j][...] = nt_dot(left_in[j][...], inverse[j], HIGHEST)
 
     def run(name, value):
         parts = range(3 * value, 3 * value + 3)
@@ -492,6 +531,19 @@
                 eliminate(piece)
             if value == 7:
                 basis_all()
+        elif name == "norms":
+            (swap_norms, finish_norms)[value]()
+        elif name == "sent":
+            for load in weight_loads:
+                load.wait()
+            for copy in started:
+                copy.wait_send()
+            started.clear()
+            for k in range(N_PARTS):
+                wait_all(partial[k].at[0:60], send_sem.at[k, 0])
+                wait_all(pairs[k], send_sem.at[k, 2])
+                wait_all(pairs[k], send_sem.at[k, 3])
+            wait_all(norms.at[0:9], norm_send.at[0])
         for k in parts:
             if name == "R1a":
                 factor_part(k)
@@ -521,32 +573,21 @@
                 gather_relay(k, 1)
             elif name == "G1c":
                 gather_finish(k, 1)
-                add_squares(k)
 
     pl.semaphore_wait(barrier, len(peers))
     for name, value in PLAN:
         run(name, value)
-    rows = [jnp.sum(value, axis=0, keepdims=True) for value in sums]
-    squares_in[0] = jnp.concatenate(rows + [jnp.zeros((5, RANK), F32)], axis=0)
-    copy = misc(16, squares_in.at[0], squares_in.at[1], partner)
-    for load in weight_loads:
-        load.wait()
-    for k in range(N_PARTS):
-        wait_all(partial[k].at[0:60], send_sem.at[k, 0])
-        wait_all(pairs[k], send_sem.at[k, 2])
-        wait_all(pairs[k], send_sem.at[k, 3])
-        wait_all(partial[k].at[0:60], send_sem.at[k, 1])
-    copy.wait_recv()
-    squares[...] = squares_in[0] + squares_in[1]
     for copy in started:
         copy.wait_send()
+    for k in range(N_PARTS):
+        wait_all(partial[k].at[0:60], send_sem.at[k, 1])
 
 
 def update_kernel(
     weight_in,
     factor,
     buffer,
-    basis,
+    rows_in,
     squares,
     moment_out,
     weight_out,
@@ -556,24 +597,9 @@
     weight_box,
     right_box,
     change_box,
-    rows_in,
     store_sem,
 ):
     scale = 1.0 / (jnp.sqrt(squares[...]) + EPSILON)
-    for j in range(3):
-        rows, pad = ROWS[j], PADDED[j]
-        value = basis[j][...]
-        if pad > rows:
-            value = jnp.concatenate([value, jnp.zeros((pad - rows, RANK), F32)], axis=0)
-        step_size = LEARN_RATE * math.sqrt(SHAPE[j][0] / SHAPE[j][1])
-        high, low = split(value * (scale[j : j + 1] * step_size))
-        rows_in[j][0:pad, 0:RANK] = high
-        rows_in[j][0:pad, RANK:] = high
-        rows_in[j][pad : 2 * pad, 0:RANK] = low
-        rows_in[j][pad : 2 * pad, RANK:] = jnp.zeros((pad, RANK), BF16)
-        moment = (value * (1.0 - DECAY)).astype(BF16)
-        rows_in[j][2 * pad :, 0:RANK] = moment
-        rows_in[j][2 * pad :, RANK:] = jnp.zeros((pad, RANK), BF16)
     where = {unit: (k, slot) for k, part in enumerate(PARTS) for slot, unit in enumerate(part)}
     for j, units in GROUPS:
         rows, pad = ROWS[j], PADDED[j]
@@ -627,9 +653,9 @@
 
     factor_shapes = [jax.ShapeDtypeStruct((64, HEIGHT[k], RANK), F32) for k in range(N_PARTS)]
     buffer_shapes = [jax.ShapeDtypeStruct((ROWS[j], COLS[j]), F32) for j in range(3)]
-    basis_shapes = [jax.ShapeDtypeStruct((ROWS[j], RANK), F32) for j in range(3)]
+    rows_shapes = [jax.ShapeDtypeStruct((3 * PADDED[j], 2 * RANK), BF16) for j in range(3)]
     weight_shapes = [jax.ShapeDtypeStruct((ROWS[j], COLS[j]), BF16) for j in range(3)]
-    middle = [factor_shapes, buffer_shapes, basis_shapes, jax.ShapeDtypeStruct((8, RANK), F32), weight_shapes]
+    middle = [factor_shapes, buffer_shapes, rows_shapes, jax.ShapeDtypeStruct((8, RANK), F32), weight_shapes]
     placed = jax.tree.map(lambda s: vmem(s.shape, s.dtype), middle)
     terms_cols = [UNIT * count for count in UNITS]
     middle = pl.pallas_call(
@@ -659,12 +685,16 @@
             vmem((3, RANK, 2 * RANK), F32),
             vmem((3, RANK, RANK), F32),
             vmem((3, 2 * RANK, RANK), BF16),
+            [vmem((PADDED[j], RANK), F32) for j in range(3)],
+            vmem((12, 8, RANK), F32),
             vmem((2, 8, RANK), F32),
             dma((3, 4, 3)),
             dma((N_PARTS, 4)),
             dma((N_PARTS, 14)),
             dma((17,)),
             dma((17,)),
+            dma((1,)),
+            dma((3,)),
         ],
         compiler_params=pltpu.CompilerParams(
             collective_id=0, has_side_effects=True, vmem_limit_bytes=45 * 2**20
@@ -672,7 +702,7 @@
         name="reduce",
     )(momentum, gradient, right, weight)
     keep = lambda x: pltpu.with_memory_space_constraint(x, vmem)
-    factor, buffer, basis, squares, weight = jax.tree.map(keep, tuple(middle))
+    factor, buffer, rows_in, squares, weight = jax.tree.map(keep, tuple(middle))
     matrices = lambda dtype: [jax.ShapeDtypeStruct((ROWS[j], COLS[j]), dtype) for j in range(3)]
     factors = [jax.ShapeDtypeStruct((COLS[j], RANK), F32) for j in range(3)]
     results = [matrices(F32), matrices(BF16), factors, matrices(F32)]
@@ -686,12 +716,11 @@
             [vmem((ROWS[j], COLS[j]), BF16) for j in range(3)],
             [vmem((COLS[j], RANK), F32) for j in range(3)],
             [vmem((ROWS[j], COLS[j]), F32) for j in range(3)],
-            [vmem((3 * PADDED[j], 2 * RANK), BF16) for j in range(3)],
             dma((3, 4)),
         ],
         compiler_params=pltpu.CompilerParams(vmem_limit_bytes=40 * 2**20),
         name="update",
-    )(weight, factor, buffer, basis, squares)
+    )(weight, factor, buffer, rows_in, squares)
     pick = lambda group: (group[1], group[2], group[0])
     return (*pick(moment), *pick(weight), *pick(right), *pick(change))
 

time: 84 us -> 80.8 us (0.962); the launches traced: 82.6 us -> 80.6 us
  Pallas kernels: 81.8 us -> 79.8 us
    pallas_call x1, Pallas kernels: 74.9 us -> 72.7 us  [local(): pl.pallas_call(reduce_kernel, out_shape=placed, in_specs=[[anywhere] * 3]...]
where the time goes in v4:
time: 80.8 us; the launch traced here: 80.6 us
  Pallas kernels  79.8 us (99%)
  between operations  0.84 us (1%)
    pallas_call x1, Pallas kernels, local(): pl.pallas_call(reduce_kernel, out_shape=placed, in_specs=[[anywhere] * 3]...  72.7 us
    pallas_call x1, Pallas kernels, local(): pl.pallas_call(update_kernel, out_shape=results, in_specs=[[inside] * 3,...  7.1 us

profile of v4, /device:TPU:0, one launch (start us, length us, event | category | flops | bytes accessed | tf_op | source)
XLA Modules:
  0.0 80.6 jit_solution(9583403142656587152)
XLA Ops:
  0.6 72.7 %reduce.1 = (f32[64,24,128]{2,1,0:T(8,128)S(1)}, f32[64,24,128]{2,1,0:T(8,128)S(1)}, f32[64,24,128]{2,1,0:T(8,128)S(1)}, f32[64,24,128]{2,1,0:T(8,128)S(1)}, f32...) custom-call(f32[216,2560]{1,0:T(8,128)} %momentum_0_.1, ...), custom_call_target="tpu_custom_call" | custom-call | tf_op jit(solution)/shard_map/reduce/pallas_call | solution.py:661
  73.4 7.1 %update.1 = (f32[216,2560]{1,0:T(8,128)}, f32[80,2560]{1,0:T(8,128)}, f32[80,6912]{1,0:T(8,128)}, bf16[216,2560]{1,0:T(8,128)(2,1)}, bf16[80,2560]{1,0:T(8,128)(...) custom-call(bf16[216,2560]{1,0:T(8,128)(2,1)S(1)} %get-tuple-element, ...), custom_call_target="tpu_custom_call" | custom-call | tf_op jit(solution)/shard_map/update/pallas_call | solution.py:709

commit v5 on v4

--- a/solution.py
+++ b/solution.py
@@ -245,6 +245,8 @@
         left[j][...] = total
         if terms[j].shape[1] > COLS[j]:
             terms[j][:, COLS[j] :] = jnp.zeros((3 * pad, terms[j].shape[1] - COLS[j]), BF16)
+        if j == 0:
+            pl.semaphore_wait(barrier, len(peers))
         return misc(j, left[j], left_in[j], partner)
 
     def left_finish(j, copy):
@@ -574,7 +576,6 @@
             elif name == "G1c":
                 gather_finish(k, 1)
 
-    pl.semaphore_wait(barrier, len(peers))
     for name, value in PLAN:
         run(name, value)
     for copy in started:

time: 80.8 us -> 80.5 us (level)
  no operation moved by 1% of the time
where the time goes in v5:
time: 80.5 us; the launch traced here: 80.4 us
  Pallas kernels  79.5 us (99%)
  between operations  0.84 us (1%)
    pallas_call x1, Pallas kernels, local(): pl.pallas_call(reduce_kernel, out_shape=placed, in_specs=[[anywhere] * 3]...  72.4 us
    pallas_call x1, Pallas kernels, local(): pl.pallas_call(update_kernel, out_shape=results, in_specs=[[inside] * 3,...  7.1 us

profile of v5, /device:TPU:0, one launch (start us, length us, event | category | flops | bytes accessed | tf_op | source)
XLA Modules:
  0.0 80.4 jit_solution(4079553860731286467)
XLA Ops:
  0.6 72.4 %reduce.1 = (f32[64,24,128]{2,1,0:T(8,128)S(1)}, f32[64,24,128]{2,1,0:T(8,128)S(1)}, f32[64,24,128]{2,1,0:T(8,128)S(1)}, f32[64,24,128]{2,1,0:T(8,128)S(1)}, f32...) custom-call(f32[216,2560]{1,0:T(8,128)} %momentum_0_.1, ...), custom_call_target="tpu_custom_call" | custom-call | tf_op jit(solution)/shard_map/reduce/pallas_call | solution.py:662
  73.1 7.1 %update.1 = (f32[216,2560]{1,0:T(8,128)}, f32[80,2560]{1,0:T(8,128)}, f32[80,6912]{1,0:T(8,128)}, bf16[216,2560]{1,0:T(8,128)(2,1)}, bf16[80,2560]{1,0:T(8,128)(...) custom-call(bf16[216,2560]{1,0:T(8,128)(2,1)S(1)} %get-tuple-element, ...), custom_call_target="tpu_custom_call" | custom-call | tf_op jit(solution)/shard_map/update/pallas_call | solution.py:710
